TPU v7x, 32 devices: a whole 2x2x4 slice. The times are simulated.
32 devices in a mesh: half: 2 (over core), dp: 2 (over x), expert: 8 (over z, y).
Axes of the slice: x: 2, y: 2, z: 4, core: 2. Of those that a mesh axis runs over, the one named last changes fastest.
Arguments:
- tokens: bfloat16 [2, 32, 128, 1024], P('half', ('dp', 'expert')), may hold values from -6 to 6
- cotangent: bfloat16 [2, 32, 128, 1024], P('half', ('dp', 'expert')), may hold values from -6 to 6
- lengths: int32 [2, 32], P(None, ('dp', 'expert')), may hold values from 64 to 128
- routes: int32 [2, 32, 128, 2], P('half', ('dp', 'expert')), may hold values from 0 to 7, all different within a row
- self_qkv: bfloat16 [2, 1024, 3072], P('half'), may hold values from -0.1875 to 0.1875
- self_out: bfloat16 [2, 1024, 1024], P('half'), may hold values from -1 to 1
- cross_weights: bfloat16 [2, 1024, 2048], P('half')
- router: bfloat16 [2, 1024, 8], P('half'), may hold values from -0.125 to 0.125
- gains: float32 [2, 3, 1024], P('half'), may hold values from 0.5 to 1.5
- bias_table: float32 [2, 512], P('half'), may hold values from -4 to 4
- expert_in: bfloat16 [2, 8, 2, 1024, 2816], P('half', 'expert'), may hold values from -0.1875 to 0.1875
- expert_out: bfloat16 [2, 8, 2816, 1024], P('half', 'expert'), may hold values from -0.21875 to 0.21875
Outputs:
- outputs: bfloat16 [2, 32, 128, 1024], P('half', ('dp', 'expert'))
- d_tokens: bfloat16 [2, 32, 128, 1024], P('half', ('dp', 'expert'))
- d_self_qkv: float32 [2, 1024, 3072], P('half', ('dp', 'expert'))
- d_self_out: float32 [2, 1024, 1024], P('half', ('dp', 'expert'))
- d_cross: float32 [2, 1024, 2048], P('half', ('dp', 'expert'))
- d_router: float32 [2, 1024, 8], P('half', ('dp', 'expert'))
- d_gains: float32 [2, 3, 1024], P('half', None, ('dp', 'expert'))
- d_bias_table: float32 [2, 512], P('half', ('dp', 'expert'))
- d_expert_in: float32 [2, 8, 2, 1024, 2816], P('half', 'expert', None, None, 'dp')
- d_expert_out: float32 [2, 8, 2816, 1024], P('half', 'expert', 'dp')
- counts: int32 [2, 2, 8], P('half', 'dp', 'expert')
Inputs may be any that keep to these rules, and one draw needn't show every extreme that they name: `routes`: the 2 experts of a token differ.
All inputs are finite; a program needn't handle non-finite values.
Results may differ from a plain program's by a relative error of at most 0.023.
Values may be sent and summed in bfloat16 or wider, within the bound.
A program may use at most 640 MiB of HBM per device.

v0:
```python
import functools

import jax
import jax.numpy as jnp
import numpy as np
from jax import lax
from jax.experimental import pallas as pl
from jax.experimental.pallas import tpu as pltpu
from jax.sharding import PartitionSpec as P

H = 16
BUCKETS = 32
EPS = 1e-06
ENC_STEPS = (12, 16, 23, 32, 46, 64, 91)
DEC_STEPS = (19, 21, 24, 27, 31, 35, 40, 46, 52, 59, 67, 77, 87, 99, 113)
F32 = jnp.float32
BF16 = jnp.bfloat16
MESH = pl.DeviceIdType.MESH
LOCAL_VMEM = 32 << 20


def cost(gigaflops):
    return pl.CostEstimate(flops=int(gigaflops * 1e9), bytes_accessed=1 << 20, transcendentals=0)
NT = (((1,), (1,)), ((), ()))
TN = (((0,), (0,)), ((), ()))


def dot(a, b, dims=(((1,), (0,)), ((), ()))):
    return lax.dot_general(a, b, dims, preferred_element_type=F32)


def diagonal_buckets(diff):
    apart = np.abs(diff)
    coarse = 8 + sum((apart >= step).astype(np.int32) for step in ENC_STEPS)
    enc = np.where(apart < 8, apart, coarse) + 16 * (diff > 0)
    behind = np.maximum(-diff, 0)
    coarse = 16 + sum((behind >= step).astype(np.int32) for step in DEC_STEPS)
    dec = np.where(behind < 16, behind, coarse)
    return enc.astype(np.int32), dec.astype(np.int32)


def diagonals(bias_ref, head, length):
    row = jnp.broadcast_to(bias_ref[pl.ds(head, 1), :], (length, 2 * length))
    return pltpu.roll(row, 0, 1, stride=1, stride_axis=0)[:, :length]


def fill_masks(info, mask_ref):
    seqs, length, _ = mask_ref.shape
    row_id = lax.broadcasted_iota(jnp.int32, (length, length), 0)
    col_id = lax.broadcasted_iota(jnp.int32, (length, length), 1)
    reach = jnp.where(info[seqs] > 0, row_id, length)
    for seq in range(seqs):
        allowed = (col_id < info[seq]) & (col_id <= reach)
        mask_ref[seq] = jnp.where(allowed, 0.0, -1000000000.0)


def attend(info, bias_ref, q_ref, k_ref, v_ref, out_ref, log_ref, mask_ref):
    has_bias = bias_ref is not None
    seqs, length, _ = mask_ref.shape
    low = lax.broadcasted_iota(jnp.int32, (length, 128), 1) < 64
    fill_masks(info, mask_ref)

    @pl.loop(0, q_ref.shape[1] // 128, unroll=4)
    def _(pair):
        cols = pl.ds(pl.multiple_of(pair * 128, 128), 128)
        biases = [diagonals(bias_ref, 2 * pair + side, length) if has_bias else 0.0 for side in range(2)]
        for seq in range(seqs):
            rows = pl.ds(seq * length, length)
            q, k, v = q_ref[rows, cols] * 0.125, k_ref[rows, cols], v_ref[rows, cols]
            mixed, peaks = [], []
            for side in range(2):
                mine = low if side == 0 else jnp.logical_not(low)
                part = jnp.where(mine, q, jnp.zeros_like(q))
                scores = dot(part, k, NT) + (mask_ref[seq] + biases[side])
                peak = jnp.max(scores, axis=-1, keepdims=True)
                spread = jnp.exp(scores - peak).astype(BF16)
                mixed.append(dot(spread, jnp.where(mine, v, jnp.ones_like(v))))
                peaks.append(peak)
            total = pltpu.roll(jnp.where(low, mixed[1], mixed[0]), 64, 1)
            out_ref[rows, cols] = (jnp.where(low, mixed[0], mixed[1]) / total).astype(BF16)
            log_ref[rows, cols] = jnp.where(low, peaks[0], peaks[1]) + jnp.log(total)


def attend_back(info, bias_ref, q_ref, k_ref, v_ref, a_ref, log_ref, g_ref, dq_ref, dkv_ref, shift, diag_ref, mask_ref):
    has_bias = bias_ref is not None
    seqs, length, _ = mask_ref.shape
    width = q_ref.shape[1]
    low = lax.broadcasted_iota(jnp.int32, (length, 128), 1) < 64
    fill_masks(info, mask_ref)
    if has_bias:
        row_id = lax.broadcasted_iota(jnp.int32, (length, length), 0)
        col_id = lax.broadcasted_iota(jnp.int32, (length, length), 1)
        flip = (row_id + col_id == length - 1).astype(F32).astype(BF16)

    @pl.loop(0, width // 128, unroll=4)
    def _(pair):
        cols = pl.ds(pl.multiple_of(pair * 128, 128), 128)
        kcols = pl.ds(pl.multiple_of(shift + pair * 128, 128), 128)
        vcols = pl.ds(pl.multiple_of(shift + width + pair * 128, 128), 128)
        biases = [diagonals(bias_ref, 2 * pair + side, length) if has_bias else 0.0 for side in range(2)]
        sums = [0.0, 0.0]
        for seq in range(seqs):
            rows = pl.ds(seq * length, length)
            q, k, v, g = q_ref[rows, cols] * 0.125, k_ref[rows, cols], v_ref[rows, cols], g_ref[rows, cols]
            logs = log_ref[rows, cols]
            turned = pltpu.roll(logs, 64, 1)
            product = g.astype(F32) * a_ref[rows, cols].astype(F32)
            minus = (-pltpu.roll(product, 64, 1)).astype(BF16)
            scaled = k * 0.125
            dqs, dks, dvs = [], [], []
            for side in range(2):
                mine = low if side == 0 else jnp.logical_not(low)
                part = jnp.where(mine, q, jnp.zeros_like(q))
                scores = dot(part, k, NT) + (mask_ref[seq] + biases[side])
                probs = jnp.exp(scores - jnp.where(mine, logs, turned))
                dvs.append(dot(probs.astype(BF16), g, TN))
                centred = dot(jnp.where(mine, g, minus), jnp.where(mine, v, jnp.ones_like(v)), NT)
                dlow = (probs * centred).astype(BF16)
                dqs.append(dot(dlow, scaled))
                dks.append(dot(dlow, q, TN))
                if has_bias:
                    sums[side] = sums[side] + dlow.astype(F32)
            dq_ref[rows, cols] = jnp.where(low, dqs[0], dqs[1]).astype(BF16)
            dkv_ref[rows, kcols] = jnp.where(low, dks[0], dks[1]).astype(BF16)
            dkv_ref[rows, vcols] = jnp.where(low, dvs[0], dvs[1]).astype(BF16)
        if has_bias:
            for side in range(2):
                upside = dot(flip, sums[side].astype(BF16))
                wide = jnp.concatenate([upside, jnp.zeros((length, length), F32)], axis=1)
                turned = pltpu.roll(wide, 0, 1, stride=1, stride_axis=0)
                diag_ref[pl.ds(2 * pair + side, 1), :] = jnp.sum(turned, axis=0, keepdims=True)


def norm_parts(values, gain):
    scale = lax.rsqrt(jnp.mean(values * values, axis=-1, keepdims=True) + EPS)
    return values * scale * gain, scale


def norm_back(values, scale, gain, grad):
    unit = values * scale
    gain_grad = jnp.sum(grad * unit, axis=0)
    pushed = grad * gain
    back = scale * (pushed - unit * jnp.mean(pushed * unit, axis=-1, keepdims=True))
    return back, gain_grad


def gelu_parts(gate):
    c, a = 0.7978845608028654, 0.044715
    square = gate * gate
    u = 0.5 + 0.5 * jnp.tanh(gate * (c + c * a * square))
    slope = u * (1.0 + (gate * (2.0 * c + 6.0 * c * a * square)) * (1.0 - u))
    return gate * u, slope


def flipped(value, bit):
    step = 1 << bit
    return value + step * (1 - 2 * (value // step % 2))


def crossed(value, other):
    for bit in range(other.bit_length()):
        if other >> bit & 1:
            value = flipped(value, bit)
    return value


def greet(partners):
    barrier = pltpu.get_barrier_semaphore()
    for partner in partners:
        pl.semaphore_signal(barrier, inc=1, device_id=partner, device_id_type=MESH)
    pl.semaphore_wait(barrier, len(partners))


def remote(src, dst, out_sem, in_sem, device):
    return pltpu.make_async_remote_copy(
        src_ref=src,
        dst_ref=dst,
        send_sem=out_sem,
        recv_sem=in_sem,
        device_id=device,
        device_id_type=MESH,
    )


def tile_loop(count, step, body):
    @pl.loop(0, count // step)
    def _(i):
        body(pl.multiple_of(i * step, step), step)

    if count % step:
        body(count // step * step, count % step)


def groups_of(experts, block):
    size = 1
    while size * 2 * block <= 320 and size * 2 <= experts:
        size *= 2
    if experts <= 2 * size:
        half = max(size // 2, 1)
        return [(0, size), *((k, half) for k in range(size, experts, half))]
    return [(k, size) for k in range(0, experts, size)]


class Turn:
    def __init__(self, experts, block, there, home):
        self.me, self.dp = lax.axis_index("expert"), lax.axis_index("dp")
        self.experts, self.block = experts, block
        self.peer = {"dp": 1 - self.dp}
        self.groups = groups_of(experts, block)
        self.there_refs, self.home_refs = there, home

    def greet(self):
        greet([{"expert": crossed(self.me, k)} for k in range(1, self.experts)] + [self.peer])

    def there(self, k):
        src, dst, out_sems, in_sems = self.there_refs
        partner = crossed(self.me, k)
        return remote(src.at[partner], dst.at[self.me], out_sems.at[k], in_sems.at[k], {"expert": partner})

    def home(self, k):
        src, dst, out_sems, in_sems = self.home_refs
        partner = crossed(self.me, k)
        return remote(src.at[partner], dst.at[self.me], out_sems.at[k], in_sems.at[k], {"expert": partner})

    def arrive(self, first, size):
        for k in range(max(first, 1), first + size):
            self.there(k).wait_recv()

    def base(self, first, size):
        return crossed(self.me // size, first // size) * size

    def spans(self, first, size):
        base = self.base(first, size)
        rows = pl.ds(pl.multiple_of(base * self.block, size * self.block), size * self.block)
        return pl.ds(base, size), rows


def every_other(width, own, parity):
    row = lax.broadcasted_iota(jnp.int32, (width, width // 2), 0)
    col = lax.broadcasted_iota(jnp.int32, (width, width // 2), 1)
    return (row == (2 * (col // own) + parity) * own + col % own).astype(F32).astype(BF16)


class Lefts:
    def __init__(self, refs, out, scratch, width, experts):
        self.me, self.own, self.width = lax.axis_index("expert"), width // (2 * experts), width
        self.refs, self.out = refs, out
        self.held, self.stage, self.loaded, self.sent, self.came = scratch
        self.half = width // 2
        self.dp = lax.axis_index("dp")

    def fetch(self, i):
        return pltpu.make_async_copy(self.refs[i], self.held.at[i % 2], self.loaded.at[i])

    def copy(self, i):
        device = {"dp": 1 - self.dp} if i < 2 else {"expert": flipped(self.me, 0)}
        return remote(self.stage.at[i], self.out.at[i], self.sent.at[i], self.came.at[i], device)

    def load(self):
        for i in range(2):
            self.fetch(i).start()

    def send(self):
        for i in range(4):
            self.fetch(i).wait()
            slot = i % self.held.shape[0]
            if i < 2:
                cols = pl.ds(pl.multiple_of((1 - self.dp) * self.half, 128), self.half)
                self.stage[i] = self.held[slot, :, cols]
            else:
                picked = every_other(self.width, self.own, 1 - self.me % 2)
                self.stage[i] = dot(self.held[slot], picked).astype(BF16)
            self.copy(i).start()
            if i + 2 < 4:
                self.fetch(i + 2).start()

    def wait(self):
        for i in range(4):
            self.copy(i).wait()


def transpose_kernel_part(loads, tall, wide, wsem, tsem):
    copies = [pltpu.make_async_copy(src, dst, wsem.at[i]) for i, (src, dst, _) in enumerate(loads)]
    for copy in copies:
        copy.start()
    for i, (_, held, out) in enumerate(loads):
        slab = tall.shape[1]
        stages = [tall.at[i] if out.shape[1] == tall.shape[2] else wide.at[pl.ds(i * slab, slab)] for i in range(2)]
        steps = out.shape[0] // slab
        copies[i].wait()

        def put(t, slot, stages=stages, out=out, slab=slab):
            rows = pl.ds(pl.multiple_of(t * slab, slab), slab)
            return pltpu.make_async_copy(stages[slot], out.at[rows], tsem.at[slot])

        def step(pair, carry, stages=stages, held=held, put=put, slab=slab, steps=steps):
            for slot in range(2):
                t = 2 * pair + slot

                @pl.when(t < steps)
                def _(t=t, slot=slot):
                    @pl.when(pair > 0)
                    def _():
                        put(t - 2, slot).wait()

                    cols = pl.ds(pl.multiple_of(t * slab, slab), slab)
                    stages[slot][...] = jnp.transpose(held[:, cols])
                    put(t, slot).start()

            return carry

        lax.fori_loop(0, pl.cdiv(steps, 2), step, 0)
        for t in (steps - 2, steps - 1):
            put(t, t % 2).wait()


def expert_forward_kernel(turn, has_prev, *refs):
    send_ref, w_in, w_down = refs[:3]
    left_refs, refs = refs[3 + 10 * has_prev : 3 + 14 * has_prev], refs[3 + 14 * has_prev :]
    back_out, rows_out, slope_out, value_out, hidden_out, slope_peer_out, value_peer_out = refs[:7]
    wgt_out, wut_out, wdt_out = refs[7:10]
    left_out, refs = refs[10 : 10 + has_prev], refs[10 + has_prev :]
    wg, wu, wd, rows, back, made, rows_peer, slopes, values, hidden = refs[:10]
    slopes_peer, values_peer, tall = refs[10:13]
    wsem, s1, r1, s2, r2, sx, rx, osem, tsem = refs[13:22]
    experts, block, width = send_ref.shape
    ff = wd.shape[0]
    span = ff // 2
    lefts = Lefts(left_refs, left_out[0], (tall, *refs[22:]), width, experts) if has_prev else None

    @pl.when(lax.axis_index("half") != turn)
    def _():
        if lefts:
            lefts.load()
            greet([{"dp": 1 - lax.axis_index("dp")}, {"expert": flipped(lax.axis_index("expert"), 0)}])
            lefts.send()
        loads = ((w_in.at[0], wg, wgt_out), (w_in.at[1], wu, wut_out), (w_down, wd, wdt_out))
        transpose_kernel_part(loads, tall, slopes, wsem, tsem)
        if lefts:
            lefts.wait()

    @pl.when(lax.axis_index("half") == turn)
    def _():
        t = Turn(experts, block, (send_ref, rows, s1, r1), (made, back, s2, r2))
        t.greet()

        def rows_over(part):
            blocks, _ = t.spans(*t.groups[part])
            return remote(rows.at[blocks], rows_peer.at[blocks], sx.at[part], rx.at[part], t.peer)

        for k in range(1, experts):
            t.there(k).start()
        rows[t.me] = send_ref[t.me]
        loads = [
            pltpu.make_async_copy(src, dst, wsem.at[i])
            for i, (src, dst) in enumerate(((w_in.at[0], wg), (w_in.at[1], wu), (w_down, wd)))
        ]
        for load in loads:
            load.start()
        if lefts:
            lefts.load()
        for part, (first, size) in enumerate(t.groups):
            t.arrive(first, size)
            rows_over(part).start()
            blocks, span_rows = t.spans(first, size)
            if part == 0:
                loads[0].wait()
                loads[1].wait()

            def up_tile(start, count, blocks=blocks, span_rows=span_rows, size=size):
                x = rows[blocks].reshape(size * block, width)
                cols = pl.ds(start, count)
                value, slope = gelu_parts(dot(x, wg[:, cols]))
                up = dot(x, wu[:, cols])
                hidden[span_rows, cols] = (value * up).astype(BF16)
                values[span_rows, cols] = value.astype(BF16)
                slopes[span_rows, cols] = (up * slope).astype(BF16)

            tile_loop(ff, 512, up_tile)
            if part == 0:
                loads[2].wait()

            def down_tile(start, count, blocks=blocks, span_rows=span_rows, size=size):
                cols = pl.ds(start, count)
                y = dot(hidden[span_rows, :], wd[:, cols]).astype(BF16)
                made[blocks, :, cols] = y.reshape(size, block, count)

            tile_loop(width, 512, down_tile)
            for k in range(max(first, 1), first + size):
                t.home(k).start()
        back[t.me] = made[t.me]
        half_cols = pl.ds(pl.multiple_of(t.dp * span, 128), span)
        other_cols = pl.ds(pl.multiple_of((1 - t.dp) * span, 128), span)
        outs = [
            (slopes, slope_out),
            (values, value_out),
            (hidden.at[:, half_cols], hidden_out.at[0]),
            (rows, rows_out.at[0]),
        ]
        outs = [pltpu.make_async_copy(src, dst, osem.at[i]) for i, (src, dst) in enumerate(outs)]
        for out in outs:
            out.start()
        if lefts:
            lefts.send()

        for part in range(len(t.groups)):
            rows_over(part).wait_recv()

        def peer_tile(start, count):
            x = rows_peer[...].reshape(experts * block, width)
            here = pl.ds(start, count)
            cols = pl.ds(pl.multiple_of(t.dp * span + start, 128), count)
            value, slope = gelu_parts(dot(x, wg[:, cols]))
            up = dot(x, wu[:, cols])
            hidden[:, pl.ds(pl.multiple_of((1 - t.dp) * span + start, 128), count)] = (value * up).astype(BF16)
            values_peer[:, here] = value.astype(BF16)
            slopes_peer[:, here] = (up * slope).astype(BF16)

        tile_loop(span, 512, peer_tile)
        more = [
            (slopes_peer, slope_peer_out),
            (values_peer, value_peer_out),
            (hidden.at[:, other_cols], hidden_out.at[1]),
            (rows_peer, rows_out.at[1]),
        ]
        more = [pltpu.make_async_copy(src, dst, osem.at[4 + i]) for i, (src, dst) in enumerate(more)]
        for out in more:
            out.start()
        for k in range(1, experts):
            t.home(k).wait_recv()
        back_copy = pltpu.make_async_copy(back, back_out, osem.at[8])
        back_copy.start()
        for k in range(1, experts):
            t.there(k).wait_send()
            t.home(k).wait_send()
        for part in range(len(t.groups)):
            rows_over(part).wait_send()
        if lefts:
            lefts.wait()
        for out in [*outs, *more, back_copy]:
            out.wait()


def expert_backward_kernel(turn, has_prev, *refs):
    send_ref = refs[0]
    sources = refs[1:8]
    refs = refs[8 + 3 * has_prev :]
    back_out, mixed_out, grad_out = refs[:3]
    wdt, dgate, dup, wgt, wut, dgate_peer, dup_peer = refs[3:10]
    grads, back, made, grads_peer = refs[10:14]
    wsem, s1, r1, s2, r2, sx, rx, osem = refs[14:]
    experts, block, width = send_ref.shape
    ff = wdt.shape[1]
    span = ff // 2
    dp = lax.axis_index("dp")
    t = Turn(experts, block, (send_ref, grads, s1, r1), (made, back, s2, r2))

    @pl.when(lax.axis_index("half") == turn)
    def _():
        t.greet()

        def grads_over(part):
            blocks, _ = t.spans(*t.groups[part])
            return remote(grads.at[blocks], grads_peer.at[blocks], sx.at[part], rx.at[part], t.peer)

        for k in range(1, experts):
            t.there(k).start()
        grads[t.me] = send_ref[t.me]
        held = (wdt, dgate, dup, wgt, wut, dgate_peer, dup_peer)
        loads = [pltpu.make_async_copy(src, dst, wsem.at[i]) for i, (src, dst) in enumerate(zip(sources, held))]
        for load in loads:
            load.start()
        for load in loads[:3]:
            load.wait()
        for part, (first, size) in enumerate(t.groups):
            t.arrive(first, size)
            grads_over(part).start()
            blocks, span_rows = t.spans(first, size)

            def hidden_tile(start, count, blocks=blocks, span_rows=span_rows, size=size):
                dy = grads[blocks].reshape(size * block, width)
                cols = pl.ds(start, count)
                dhidden = dot(dy, wdt[:, cols])
                dgate[span_rows, cols] = (dhidden * dgate[span_rows, cols].astype(F32)).astype(BF16)
                dup[span_rows, cols] = (dhidden * dup[span_rows, cols].astype(F32)).astype(BF16)

            tile_loop(ff, 512, hidden_tile)
            if part == 0:
                loads[3].wait()
                loads[4].wait()

            def rows_tile(start, count, blocks=blocks, span_rows=span_rows, size=size):
                cols = pl.ds(start, count)
                dr = dot(dgate[span_rows, :], wgt[:, cols]) + dot(dup[span_rows, :], wut[:, cols])
                made[blocks, :, cols] = dr.astype(BF16).reshape(size, block, count)

            tile_loop(width, 512, rows_tile)
            for k in range(max(first, 1), first + size):
                t.home(k).start()
        back[t.me] = made[t.me]
        half_cols = pl.ds(pl.multiple_of(dp * span, 128), span)
        outs = [
            (dgate.at[:, half_cols], mixed_out.at[0, 0]),
            (dup.at[:, half_cols], mixed_out.at[1, 0]),
            (grads, grad_out.at[0]),
        ]
        outs = [pltpu.make_async_copy(src, dst, osem.at[i]) for i, (src, dst) in enumerate(outs)]
        for out in outs:
            out.start()

        for load in loads[5:]:
            load.wait()
        for part in range(len(t.groups)):
            grads_over(part).wait_recv()

        def peer_tile(start, count):
            dy = grads_peer[...].reshape(experts * block, width)
            here = pl.ds(start, count)
            dhidden = dot(dy, wdt[:, pl.ds(pl.multiple_of(dp * span + start, 128), count)])
            dgate_peer[:, here] = (dhidden * dgate_peer[:, here].astype(F32)).astype(BF16)
            dup_peer[:, here] = (dhidden * dup_peer[:, here].astype(F32)).astype(BF16)

        tile_loop(span, 512, peer_tile)
        more = [
            (dgate_peer, mixed_out.at[0, 1]),
            (dup_peer, mixed_out.at[1, 1]),
            (grads_peer, grad_out.at[1]),
        ]
        more = [pltpu.make_async_copy(src, dst, osem.at[3 + i]) for i, (src, dst) in enumerate(more)]
        for out in more:
            out.start()
        for k in range(1, experts):
            t.home(k).wait_recv()
        back_copy = pltpu.make_async_copy(back, back_out, osem.at[6])
        back_copy.start()
        for k in range(1, experts):
            t.there(k).wait_send()
            t.home(k).wait_send()
        for part in range(len(t.groups)):
            grads_over(part).wait_send()
        for out in [*outs, *more, back_copy]:
            out.wait()


def expert_call(kernel, number, turn, send, sources, prev, more, out_shape, scratch, name):
    vmem, hbm = pl.BlockSpec(memory_space=pltpu.VMEM), pl.BlockSpec(memory_space=pl.ANY)
    prev = list(prev or [])
    return pl.pallas_call(
        functools.partial(kernel, turn, bool(prev)),
        in_specs=[vmem] + [hbm] * (len(sources) + len(prev) + len(more)),
        out_specs=[hbm] * len(out_shape),
        out_shape=out_shape,
        input_output_aliases={1 + len(sources) + i: i for i in range(len(prev))},
        scratch_shapes=scratch,
        compiler_params=pltpu.CompilerParams(
            collective_id=number, has_side_effects=True, vmem_limit_bytes=60 << 20
        ),
        cost_estimate=cost(40),
        name=name,
    )(send, *sources, *prev, *more)


def moe_forward(send, w_in, w_down, turn, prev, lefts, slab):
    experts, block, width = send.shape
    ff = w_down.shape[0]
    total = experts * block
    parts = len(groups_of(experts, block))
    dma = pltpu.SemaphoreType.DMA
    scratch = [
        pltpu.VMEM((width, ff), BF16),
        pltpu.VMEM((width, ff), BF16),
        pltpu.VMEM((ff, width), BF16),
        *[pltpu.VMEM(send.shape, BF16)] * 4,
        *[pltpu.VMEM((total, ff), BF16)] * 3,
        *[pltpu.VMEM((total, ff // 2), BF16)] * 2,
        pltpu.VMEM((2, slab, width), BF16),
        dma((3,)),
        *[dma((experts,))] * 4,
        *[dma((parts,))] * 2,
        dma((9,)),
        dma((2,)),
    ]
    shapes = [
        send.shape,
        (2, *send.shape),
        (total, ff),
        (total, ff),
        (2, total, ff // 2),
        (total, ff // 2),
        (total, ff // 2),
        (ff, width),
        (ff, width),
        (width, ff),
    ]
    if lefts:
        rows = lefts[0].shape[0]
        shapes.append((4, rows, width // 2))
        scratch += [pltpu.VMEM((4, rows, width // 2), BF16), *[dma((4,))] * 3]
    out_shape = [jax.ShapeDtypeStruct(shape, BF16) for shape in shapes]
    return expert_call(
        expert_forward_kernel, 1 + turn, turn, send, [w_in, w_down], prev, lefts, out_shape, scratch, "moe_forward"
    )


def moe_backward(grad_send, saved, turn, prev):
    experts, block, width = grad_send.shape
    _, _, slope, value, _, slope_peer, value_peer, wgt, wut, wdt, _ = saved
    total, ff = slope.shape
    parts = len(groups_of(experts, block))
    dma = pltpu.SemaphoreType.DMA
    scratch = [
        pltpu.VMEM((width, ff), BF16),
        *[pltpu.VMEM((total, ff), BF16)] * 2,
        *[pltpu.VMEM((ff, width), BF16)] * 2,
        *[pltpu.VMEM((total, ff // 2), BF16)] * 2,
        *[pltpu.VMEM(grad_send.shape, BF16)] * 4,
        dma((7,)),
        *[dma((experts,))] * 4,
        *[dma((parts,))] * 2,
        dma((7,)),
    ]
    out_shape = [
        jax.ShapeDtypeStruct(grad_send.shape, BF16),
        jax.ShapeDtypeStruct((2, 2, total, ff // 2), BF16),
        jax.ShapeDtypeStruct((2, *grad_send.shape), BF16),
    ]
    return expert_call(
        expert_backward_kernel,
        3 + turn,
        turn,
        grad_send,
        [wdt, slope, value, wgt, wut, slope_peer, value_peer],
        prev,
        [],
        out_shape,
        scratch,
        "moe_backward",
    )


GATE, TOTAL, SCALE, ROUTE, FIRST = 0, 2, 3, 4, 8


class Loads:
    def __init__(self, pairs, sems):
        self.copies = [pltpu.make_async_copy(src, dst, sems.at[i]) for i, (src, dst) in enumerate(pairs)]

    def start(self):
        for copy in self.copies:
            copy.start()

    def wait(self, *which):
        for i in which:
            self.copies[i].wait()


def slots_kernel(experts, capacity, block, order_ref, spots_out, both_out, turned_out, both_turned_out, tally_out, route_out, route_rows):
    seqs, pairs = order_ref.shape
    top = spots_out.shape[1] // both_out.shape[1]
    length = pairs // top
    rows = seqs * length
    slots = spots_out.shape[0]
    expert_id = lax.broadcasted_iota(jnp.int32, (experts, pairs), 0)
    slot_id = lax.broadcasted_iota(jnp.int32, (slots, length), 0)
    row_id = lax.broadcasted_iota(jnp.int32, (pairs, pairs), 0)
    col_id = lax.broadcasted_iota(jnp.int32, (pairs, pairs), 1)
    earlier = (row_id < col_id).astype(F32).astype(BF16)
    route_rows[...] = jnp.zeros_like(route_rows)
    tally = jnp.zeros((experts, 128), F32)
    lane = lax.broadcasted_iota(jnp.int32, (experts, 128), 1)
    for seq in range(seqs):
        order = order_ref[seq : seq + 1, :]
        picked = (expert_id == order).astype(F32)
        place = jnp.sum(dot(picked.astype(BF16), earlier) * picked, axis=0, keepdims=True)
        kept = place < capacity
        target = jnp.where(kept, order * block + seq * capacity + place.astype(jnp.int32), -1)
        taken = jnp.sum(picked * kept.astype(F32), axis=1, keepdims=True)
        whole = jnp.sum(picked, axis=1, keepdims=True)
        tally = tally + jnp.where(lane == 0, taken, jnp.where(lane == 1, whole, 0.0))
        total = jnp.zeros((slots, length), F32)
        for k in range(top):
            part = pl.ds(k * length, length)
            hot = (slot_id == target[:, k * length : (k + 1) * length]).astype(F32)
            spots_out[:, pl.ds(k * rows + seq * length, length)] = hot.astype(BF16)
            total = total + hot
            route_rows[pl.ds(ROUTE + k, 1), pl.ds(seq * length, length)] = order_ref[
                pl.ds(seq, 1), part
            ].astype(F32)
        both_out[:, pl.ds(seq * length, length)] = total.astype(BF16)
    tally_out[...] = tally
    turned_out[...] = jnp.transpose(spots_out[...])
    both_turned_out[...] = jnp.transpose(both_out[...])
    route_out[...] = jnp.transpose(route_rows[...])


def find_slots(order, experts, capacity, block, top):
    seqs, pairs = order.shape
    rows = seqs * pairs // top
    slots = experts * block
    vmem = pl.BlockSpec(memory_space=pltpu.VMEM)
    return pl.pallas_call(
        functools.partial(slots_kernel, experts, capacity, block),
        in_specs=[vmem],
        out_specs=[vmem] * 6,
        out_shape=[
            jax.ShapeDtypeStruct((slots, top * rows), BF16),
            jax.ShapeDtypeStruct((slots, rows), BF16),
            jax.ShapeDtypeStruct((top * rows, slots), BF16),
            jax.ShapeDtypeStruct((rows, slots), BF16),
            jax.ShapeDtypeStruct((experts, 128), F32),
            jax.ShapeDtypeStruct((rows, 128), F32),
        ],
        scratch_shapes=[pltpu.VMEM((128, rows), F32)],
        compiler_params=pltpu.CompilerParams(vmem_limit_bytes=LOCAL_VMEM),
        cost_estimate=cost(1),
        name="find_slots",
    )(order)


def enter_kernel(cross, experts, count, info, gain_ref, router_ref, lanes_ref, lead_ref, *refs):
    held, refs = refs[:count], refs[count:]
    mixed_out, log_out, result_out, stats_out, send_out, low_ref, mask_ref = refs
    w_out, x, spots = held[count - 3 :]
    rows, width = x.shape
    step = min(512, width)
    if cross:
        q_ref, kv = held[:2]
        k_ref, v_ref = kv.at[:, pl.ds(0, width)], kv.at[:, pl.ds(width, width)]
    else:
        q_ref, k_ref, v_ref = (held[0].at[:, pl.ds(i * width, width)] for i in range(3))

    def work():
        attend(info, None if cross else lead_ref, q_ref, k_ref, v_ref, mixed_out, log_out, mask_ref)
        for start in range(0, width, step):
            cols = pl.ds(start, step)
            result_out[:, cols] = x[:, cols].astype(F32) + dot(mixed_out[...], w_out[:, cols])
        values = result_out[...]
        scale = lax.rsqrt(jnp.mean(values * values, axis=-1, keepdims=True) + EPS)
        normed = values * scale * gain_ref[...]
        low = normed.astype(BF16)
        low_ref[...] = low
        logits = dot(low, router_ref[...]) + dot((normed - low.astype(F32)).astype(BF16), router_ref[...])
        lane = lax.broadcasted_iota(jnp.int32, (rows, 128), 1)
        valid = (lane >= FIRST) & (lane < FIRST + experts)
        logits = jnp.where(valid, logits, -1e30)
        spread = jnp.where(valid, jnp.exp(logits - jnp.max(logits, axis=-1, keepdims=True)), 0.0)
        probs = spread / jnp.sum(spread, axis=-1, keepdims=True)
        routes = lanes_ref[...]
        chosen = [
            jnp.sum(
                jnp.where(lane == routes[:, ROUTE + k : ROUTE + k + 1].astype(jnp.int32) + FIRST, probs, 0.0),
                axis=-1,
                keepdims=True,
            )
            for k in range(2)
        ]
        total = chosen[0] + chosen[1]
        stats = probs + routes
        for at, column in ((GATE, chosen[0] / total), (GATE + 1, chosen[1] / total), (TOTAL, total), (SCALE, scale)):
            stats = jnp.where(lane == at, column, stats)
        stats_out[...] = stats
        for start in range(0, width, step):
            cols = pl.ds(start, step)
            send_out[:, cols] = dot(spots[...], low_ref[:, cols]).astype(BF16)

    if not cross:
        work()
        return
    decoder = lax.axis_index("half") == 1
    pl.when(decoder)(work)

    @pl.when(jnp.logical_not(decoder))
    def _():
        result_out[...] = x[...].astype(F32)
        stats_out[...] = lead_ref[...]


def enter(info, gain, router, lanes, lead, cross, sources, experts, length):
    rows, width = sources[-2].shape
    vmem = pl.BlockSpec(memory_space=pltpu.VMEM)
    count = len(sources)
    return pl.pallas_call(
        functools.partial(enter_kernel, cross, experts, count),
        in_specs=[pl.BlockSpec(memory_space=pltpu.SMEM)] + [vmem] * (4 + count),
        out_specs=[vmem] * 5,
        out_shape=[
            jax.ShapeDtypeStruct((rows, width), BF16),
            jax.ShapeDtypeStruct((rows, width), F32),
            jax.ShapeDtypeStruct((rows, width), F32),
            jax.ShapeDtypeStruct((rows, 128), F32),
            jax.ShapeDtypeStruct((sources[-1].shape[0], width), BF16),
        ],
        scratch_shapes=[
            pltpu.VMEM((rows, width), BF16),
            pltpu.VMEM((rows // length, length, length), F32),
        ],
        compiler_params=pltpu.CompilerParams(vmem_limit_bytes=LOCAL_VMEM),
        cost_estimate=cost(10),
        name="enter_cross" if cross else "enter_self",
    )(info, gain, router, lanes, lead, *sources)


def norm_back_rows(values, scale, gain, grad):
    unit = values * scale
    pushed = grad * gain
    back = scale * (pushed - unit * jnp.mean(pushed * unit, axis=-1, keepdims=True))
    return back, jnp.sum(grad * unit, axis=0, keepdims=True)


def leave_kernel(cross, experts, count, info, stats_ref, gain_ref, router_ref, *refs):
    bias_ref, refs = (None, refs) if cross else (refs[0], refs[1:])
    sources, refs = refs[:count], refs[count:]
    grad_out, branch_out, dgain_out, dlog_out, dq_out, last_out = refs[:6]
    held, (dmixed, mask_ref, sems) = refs[6 : 6 + count], refs[6 + count :]
    back, both, grad, results, x, w_out, a, log = held[:8]
    seqs, length, _ = mask_ref.shape
    width = x.shape[1]
    loads = Loads(zip(sources, held), sems)
    if cross:
        q_ref, kv = held[8:]
        k_ref, v_ref = kv.at[:, pl.ds(0, width)], kv.at[:, pl.ds(width, width)]
        dkv_out, shift, diag_out = last_out, 0, None
    else:
        qkv, ready = held[8:]
        q_ref, k_ref, v_ref = (qkv.at[:, pl.ds(i * width, width)] for i in range(3))
        dkv_out, shift, diag_out = dq_out, width, last_out

    def leave():
        loads.wait(0, 1, 2, 3, 4)
        dgain = jnp.zeros((1, width), F32)
        lane = lax.broadcasted_iota(jnp.int32, (length, 128), 1)
        for seq in range(seqs):
            rows = pl.ds(seq * length, length)
            stats = stats_ref[rows, :]
            gates = [stats[:, GATE + k : GATE + k + 1] for k in range(2)]
            hots = [
                (lane == stats[:, ROUTE + k : ROUTE + k + 1].astype(jnp.int32) + FIRST).astype(F32)
                for k in range(2)
            ]
            probs = jnp.where((lane >= FIRST) & (lane < FIRST + experts), stats, 0.0)
            g = grad[rows, :].astype(F32)
            dgates = [
                jnp.sum(g * results[k, rows, :].astype(F32), axis=-1, keepdims=True) for k in range(2)
            ]
            shared = dgates[0] * gates[0] + dgates[1] * gates[1]
            dprobs = sum((dgates[k] - shared) / stats[:, TOTAL : TOTAL + 1] * hots[k] for k in range(2))
            dlog = probs * (dprobs - jnp.sum(dprobs * probs, axis=-1, keepdims=True))
            dlog_out[rows, :] = dlog
            dnormed = dot(both[rows, :], back[...]) + dot(dlog.astype(BF16), router_ref[...], NT)
            dx, part = norm_back_rows(x[rows, :], stats[:, SCALE : SCALE + 1], gain_ref[...], dnormed)
            dgain = dgain + part
            grad_out[rows, :] = g + dx
        dgain_out[...] = jnp.broadcast_to(dgain, dgain_out.shape)

    def attention():
        loads.wait(5)
        branch_out[...] = grad_out[...].astype(BF16)
        step = min(512, width)
        for start in range(0, width, step):
            cols = pl.ds(start, step)
            dmixed[:, cols] = dot(branch_out[...], w_out[cols, :], NT).astype(BF16)
        loads.wait(*((6, 7, 8, 9) if cross else (6, 7, 8)))
        attend_back(
            info, bias_ref, q_ref, k_ref, v_ref, a, log, dmixed, dq_out, dkv_out, shift, diag_out, mask_ref
        )

    decoder = lax.axis_index("half") == 1
    if cross:

        @pl.when(decoder)
        def _():
            loads.start()
            leave()
            attention()

    else:
        loads.start()

        @pl.when(jnp.logical_not(decoder))
        def _():
            leave()
            loads.wait(9)

        @pl.when(decoder)
        def _():
            loads.wait(0, 1, 2, 3, 4, 9)
            grad_out[...] = ready[...]

        attention()


def leave(info, stats, gain, router, bias, sources, experts, length):
    cross = bias is None
    rows, width = sources[4].shape
    seqs = rows // length
    vmem, hbm = pl.BlockSpec(memory_space=pltpu.VMEM), pl.BlockSpec(memory_space=pl.ANY)
    lead = [] if cross else [bias]
    out_shape = [
        jax.ShapeDtypeStruct((rows, width), F32),
        jax.ShapeDtypeStruct((rows, width), BF16),
        jax.ShapeDtypeStruct((8, width), F32),
        jax.ShapeDtypeStruct((rows, 128), F32),
        jax.ShapeDtypeStruct((rows, width if cross else 3 * width), BF16),
        jax.ShapeDtypeStruct((rows, 2 * width), BF16) if cross else jax.ShapeDtypeStruct(bias.shape, F32),
    ]
    return pl.pallas_call(
        functools.partial(leave_kernel, cross, experts, len(sources)),
        in_specs=[pl.BlockSpec(memory_space=pltpu.SMEM)] + [vmem] * (3 + len(lead)) + [hbm] * len(sources),
        out_specs=[vmem] * 6,
        out_shape=out_shape,
        scratch_shapes=[
            *(pltpu.VMEM(a.shape, a.dtype) for a in sources),
            pltpu.VMEM((rows, width), BF16),
            pltpu.VMEM((seqs, length, length), F32),
            pltpu.SemaphoreType.DMA((len(sources),)),
        ],
        compiler_params=pltpu.CompilerParams(vmem_limit_bytes=56 << 20),
        cost_estimate=cost(16),
        name="leave_cross" if cross else "leave_self",
    )(info, stats, gain, router, *lead, *sources)


def memory_kernel(stats_ref, gain_ref, *refs):
    (dmemory, w, x, cotangent, spots), parts, refs = refs[:5], refs[5:7], refs[7:]
    grad_out, send_out, dgain_out, cross_out, dnormed, spread = refs
    rows, width = x.shape

    @pl.when(lax.axis_index("half") == 1)
    def _():
        for i, part in enumerate(parts):
            cross_out[:, pl.ds(i * width, width)] = part[...]

    @pl.when(lax.axis_index("half") == 0)
    def _():
        cross_out[...] = dmemory[...]
        step = min(512, width)
        for start in range(0, width, step):
            cols = pl.ds(start, step)
            dnormed[:, cols] = dot(dmemory[...], w[cols, :], NT)
        scale = lax.rsqrt(jnp.mean(x[...] * x[...], axis=-1, keepdims=True) + EPS)
        dx, dgain = norm_back_rows(x[...], scale, gain_ref[...], dnormed[...])
        dgain_out[...] = jnp.broadcast_to(dgain, dgain_out.shape)
        grad = cotangent[...].astype(F32) + dx
        grad_out[...] = grad
        for k in range(2):
            gate = stats_ref[:, GATE + k : GATE + k + 1]
            spread[pl.ds(k * rows, rows), :] = (gate * grad).astype(BF16)
        for start in range(0, width, step):
            cols = pl.ds(start, step)
            send_out[:, cols] = dot(spots[...], spread[:, cols]).astype(BF16)


def memory_gradient(stats, gain, sources, parts):
    rows, width = sources[2].shape
    vmem = pl.BlockSpec(memory_space=pltpu.VMEM)
    return pl.pallas_call(
        memory_kernel,
        in_specs=[vmem] * (2 + len(sources) + len(parts)),
        out_specs=[vmem] * 4,
        out_shape=[
            jax.ShapeDtypeStruct((rows, width), F32),
            jax.ShapeDtypeStruct((sources[4].shape[0], width), BF16),
            jax.ShapeDtypeStruct((8, width), F32),
            jax.ShapeDtypeStruct((rows, 2 * width), BF16),
        ],
        scratch_shapes=[
            pltpu.VMEM((rows, width), F32),
            pltpu.VMEM((2 * rows, width), BF16),
        ],
        compiler_params=pltpu.CompilerParams(vmem_limit_bytes=LOCAL_VMEM),
        cost_estimate=cost(4),
        name="memory_gradient",
    )(stats, gain, *sources, *parts)


def dense_kernel(stages, chunk, lag, *refs):
    sources, small_ref = refs[:11], refs[11]
    out_refs, small_out, small_in = refs[12:15], refs[15], refs[16]
    held, xt_ref, refs = refs[17:28], refs[28], refs[29:]
    x_refs, own_refs, peer_refs, xp = held[:4], held[4:7], held[7:10], held[10]
    sums, parts = refs[:stages], refs[stages : 2 * stages]
    odd_parts, ss, rs, sk, rk, sl = refs[2 * stages :]
    counts = [ref.shape[1] // chunk for ref in own_refs]
    starts = [sum(counts[:i]) for i in range(3)]
    chunks = sum(counts)
    per_cross = counts[2] // 2
    rows, half = xp.shape[1:]
    dp, me = lax.axis_index("dp"), lax.axis_index("expert")
    peer = {"dp": 1 - dp}
    partners = [flipped(me, k) for k in range(stages)]
    bits = [me // (1 << k) % 2 for k in range(stages)]
    load = [pltpu.make_async_copy(sources[i], held[i], sl.at[i]) for i in range(11)]
    for i in (10, 2, 3, 6, 9, 0, 4, 7, 1, 5, 8):
        load[i].start()
    greet([peer] + [{"expert": p} for p in partners])

    def send_small(step):
        src = small_ref if step == 0 else small_out.at[step - 1]
        device = peer if step == 0 else {"expert": partners[stages - step]}
        return remote(src, small_in.at[step], ss.at[step], rs.at[step], device)

    eighth = odd_parts.shape[1]

    def send_part(k, c, odd):
        if k == 0 and odd:
            src = sums[0].at[c, pl.ds((1 - dp) * eighth, eighth)]
            return remote(src, odd_parts.at[c - early], sk.at[0, c], rk.at[0, c], peer)
        other = 1 - bits[k]
        src = sums[0].at[c, :, :, other] if k == 0 else sums[k].at[c, :, other]
        return remote(src, parts[k].at[c], sk.at[k, c], rk.at[k, c], {"expert": partners[k]})

    def turn_x(g):
        load[g].wait()
        if g < 2:
            cols = pl.ds(pl.multiple_of(dp * half, half), half)
            own = x_refs[g][:, cols]
        else:
            own = dot(x_refs[g][...], every_other(2 * half, out_refs[0].shape[0], bits[0])).astype(BF16)
        xt_ref[g, :, :rows] = jnp.transpose(own)
        xt_ref[g, :, rows:] = jnp.transpose(xp[g])

    def small_step(j):
        send_small(j).wait_recv()
        own = small_ref[...] if j == 0 else small_out[j - 1]
        small_out[j] = own + small_in[j]
        if j < stages:
            send_small(j + 1).start()

    send_small(0).start()
    load[10].wait()
    last = counts[2]
    early = chunks - last
    per = chunks // last

    def produce(i, carry):
        c = jnp.where(lax.rem(i, per) == 0, early + i // per, i - i // per - 1)
        for g in range(3):

            @pl.when(c == starts[g])
            def _(g=g):
                load[4 + g].wait()
                load[7 + g].wait()
                for x in (g,) if g < 2 else (2, 3):
                    turn_x(x)

            @pl.when((c >= starts[g]) & (c < starts[g] + counts[g]))
            def _(g=g):
                at = c - starts[g]
                cols = pl.ds(pl.multiple_of(at * chunk, chunk), chunk)
                which = g if g < 2 else 2 + at // per_cross
                total = dot(xt_ref[which, :, :rows], own_refs[g][:, cols])
                total += dot(xt_ref[which, :, rows:], peer_refs[g][:, cols])
                sums[0][c] = total.astype(BF16).reshape(sums[0].shape[1:])
                send_part(0, c, g == 2).start()

        for j in range(2):

            @pl.when(i == 3 + 6 * j)
            def _(j=j):
                small_step(j)

        return carry

    lax.fori_loop(0, chunks, produce, 0)

    def advance(k, c, odd):
        send_part(k, c, odd).wait_recv()
        if k == 0 and odd:
            mine, other = sums[0][c, pl.ds(dp * eighth, eighth)], odd_parts[c - early]
        else:
            mine = sums[0][c, :, :, bits[0]] if k == 0 else sums[k][c, :, bits[k]]
            other = parts[k][c]
        total = mine.astype(F32) + other.astype(F32)
        if k + 1 < stages:
            sums[k + 1][c] = total.astype(BF16).reshape(sums[k + 1].shape[1:])
            send_part(k + 1, c, odd).start()
            return
        total = total.reshape(total.shape[-2:])
        for g in (2,) if odd else (0, 1):

            @pl.when((c >= starts[g]) & (c < starts[g] + counts[g]))
            def _(g=g):
                at = pl.multiple_of((c - starts[g]) * chunk, chunk)
                out_refs[g][:, pl.ds(at, chunk)] = total

    def reduce(i, carry):
        for k in range(stages):
            c = i - lag * k

            @pl.when((c >= 0) & (c < early))
            def _(k=k, c=c):
                advance(k, c, False)

        for k in range(stages):
            twice = i - 1 - 3 * k

            @pl.when((twice >= 0) & (lax.rem(twice, 2) == 0) & (twice < 2 * last))
            def _(k=k, twice=twice):
                advance(k, early + twice // 2, True)

        for j in range(2, stages + 1):

            @pl.when(i == 3 * j - 2)
            def _(j=j):
                small_step(j)

        return carry

    steps = max(early + lag * (stages - 1), 2 * last + 3 * (stages - 1), 3 * stages - 1)
    lax.fori_loop(0, steps, reduce, 0)

    def finish(c, carry, odd):
        for k in range(stages):
            send_part(k, c, odd).wait_send()
        return carry

    lax.fori_loop(0, early, functools.partial(finish, odd=False), 0)
    lax.fori_loop(early, chunks, functools.partial(finish, odd=True), 0)
    for j in range(stages + 1):
        send_small(j).wait_send()


def to_neighbour(array):
    count = lax.axis_size("expert")
    return lax.ppermute(array, "expert", [(i, i ^ 1) for i in range(count)])


def over_dp(array):
    return lax.ppermute(array, "dp", [(0, 1), (1, 0)])


def dense_gradients(lefts, lefts_peer, own, peer, small, experts):
    chunk = 512
    rows, width = lefts[0].shape
    half_rows = width // 2
    chunks = sum(y.shape[1] for y in own) // chunk
    stages = experts.bit_length() - 1
    keep = half_rows // experts
    vmem, hbm = pl.BlockSpec(memory_space=pltpu.VMEM), pl.BlockSpec(memory_space=pl.ANY)
    dma = pltpu.SemaphoreType.DMA
    sources = [*lefts, *own, *peer, lefts_peer]
    blocks = [(experts // 4, 2, 2)] + [(experts >> (k + 1), 2) for k in range(1, stages)]
    halved = [(experts // 4, 2)] + [(experts >> (k + 1),) for k in range(1, stages)]
    scratch = [pltpu.VMEM((stages + 1, *small.shape), F32)]
    scratch += [pltpu.VMEM(a.shape, BF16) for a in sources]
    scratch += [pltpu.VMEM((4, half_rows, 2 * rows), BF16)]
    scratch += [pltpu.VMEM((chunks, *b, keep, chunk), BF16) for b in blocks + halved]
    scratch += [pltpu.VMEM((own[2].shape[1] // chunk, experts // 8, 2, 2, keep, chunk), BF16)]
    scratch += [dma((stages + 1,)), dma((stages + 1,)), dma((stages, chunks)), dma((stages, chunks))]
    scratch += [dma((len(sources),))]
    *outs, sums = pl.pallas_call(
        functools.partial(dense_kernel, stages, chunk, 2),
        in_specs=[hbm] * len(sources) + [vmem],
        out_specs=[vmem] * 4,
        out_shape=[
            *(jax.ShapeDtypeStruct((keep, y.shape[1]), F32) for y in own),
            jax.ShapeDtypeStruct((stages + 1, *small.shape), F32),
        ],
        scratch_shapes=scratch,
        compiler_params=pltpu.CompilerParams(
            collective_id=0, has_side_effects=True, vmem_limit_bytes=56 << 20
        ),
        cost_estimate=cost(45),
        name="dense_gradients",
    )(*sources, small)
    return outs, sums[stages]


def product_kernel(x_ref, y_ref, out_ref):
    out_ref[...] = dot(x_ref[...], y_ref[...].reshape(y_ref.shape[-2:]), TN).reshape(out_ref.shape)


def expert_gradients(rows, mixed, hidden, grads):
    total, width = rows.shape
    span = hidden.shape[1]
    tile = 256
    params = pltpu.CompilerParams(vmem_limit_bytes=40 << 20)
    din = pl.pallas_call(
        product_kernel,
        grid=(2, width // tile),
        in_specs=[
            pl.BlockSpec((total, tile), lambda g, i: (0, i)),
            pl.BlockSpec((1, total, span), lambda g, i: (g, 0, 0)),
        ],
        out_specs=pl.BlockSpec((1, tile, span), lambda g, i: (g, i, 0)),
        out_shape=jax.ShapeDtypeStruct((2, width, span), F32),
        compiler_params=params,
        cost_estimate=cost(12),
        name="expert_in_gradient",
    )(rows, mixed)
    ddown = pl.pallas_call(
        product_kernel,
        grid=(pl.cdiv(span, tile),),
        in_specs=[
            pl.BlockSpec((total, tile), lambda i: (0, i)),
            pl.BlockSpec((total, width), lambda i: (0, 0)),
        ],
        out_specs=pl.BlockSpec((tile, width), lambda i: (i, 0)),
        out_shape=jax.ShapeDtypeStruct((span, width), F32),
        compiler_params=params,
        cost_estimate=cost(7),
        name="expert_out_gradient",
    )(hidden, grads)
    return din, ddown


def body(
    tokens,
    cotangent,
    lengths,
    routes,
    self_qkv,
    self_out,
    cross_weights,
    router,
    gains,
    bias_table,
    expert_in,
    expert_out,
):
    _, seqs, length, width = tokens.shape
    heads = H
    experts = router.shape[2]
    top = routes.shape[3]
    capacity = (5 * top * length + 4 * experts - 1) // (4 * experts)
    block_rows = -(-seqs * capacity // 16) * 16
    rows = seqs * length
    slots = experts * block_rows
    half_index = lax.axis_index("half")
    decoder = half_index == 1
    wqkv, wout, wcross, wrouter, gain = (
        self_qkv[0],
        self_out[0],
        cross_weights[0],
        router[0],
        gains[0],
    )
    w_in, w_down = expert_in[0, 0], expert_out[0, 0]

    column = np.arange(2 * length)
    entry = np.arange(BUCKETS * heads)
    hot, hot_back = (
        jnp.where(
            decoder,
            *(
                (entry[:, None] // heads == bucket[None, :]).astype(np.float32)
                for bucket in reversed(diagonal_buckets(diff))
            ),
        )
        for diff in (np.where(column < length, column, column - 2 * length), column - length + 1)
    )
    own_head = entry[None, :] % heads == np.arange(heads)[:, None]
    bias = lax.dot_general(
        jnp.where(own_head, bias_table, 0.0),
        hot,
        (((1,), (0,)), ((), ())),
        precision=lax.Precision.HIGHEST,
        preferred_element_type=F32,
    )
    own_lengths = jnp.where(decoder, lengths[1], lengths[0])
    self_info = jnp.concatenate([own_lengths, half_index[None]]).astype(jnp.int32)
    cross_info = jnp.concatenate([lengths[0], jnp.zeros((1,), jnp.int32)]).astype(jnp.int32)

    order = jnp.transpose(routes[0], (0, 2, 1)).reshape(seqs, top * length)
    spots, both_spots, stacked, both, tally, route_lanes = find_slots(order, experts, capacity, block_rows, top)
    tallies = jnp.concatenate([tally[:, 0], tally[:, 1] - tally[:, 0]])
    router_wide = jnp.pad(wrouter, ((0, 0), (FIRST, 128 - FIRST - experts)))

    def fetch(returned):
        flat = returned.reshape(slots, width)
        return dot(stacked, flat).astype(BF16).reshape(top, rows, width)

    def combine(values, stats, results):
        return values + sum(stats[:, GATE + k : GATE + k + 1] * results[k] for k in range(top))

    values = tokens[0].reshape(rows, width).astype(F32)
    normed, scale0 = norm_parts(values, gain[0])
    low0 = normed.astype(BF16)
    qkv = dot(low0, wqkv).astype(BF16)
    mixed0, log0, first, stats, send = enter(
        self_info,
        gain[1:2],
        router_wide,
        route_lanes,
        bias,
        False,
        [qkv, wout, tokens[0].reshape(rows, width), both_spots],
        experts,
        length,
    )

    send_shape = (experts, block_rows, width)
    saved = moe_forward(send.reshape(send_shape), w_in, w_down, 0, None, [], rows)
    final_enc = combine(first, stats, fetch(saved[0]))
    normed, scale_m = norm_parts(final_enc, gain[2])
    low_m = normed.astype(BF16)
    memory = dot(low_m, wcross).astype(BF16)
    names = ("half", "dp", "expert")
    forward_pairs, back_pairs = half_pairs(lax.axis_size("dp") * lax.axis_size("expert"))
    memory = lax.ppermute(memory, names, forward_pairs)

    normed, scale_c = norm_parts(first, gain[2])
    low_c = normed.astype(BF16)
    query = dot(low_c, wcross[:, :width]).astype(BF16)
    mixed_c, log_c, second, stats, send = enter(
        cross_info,
        gain[1:2],
        router_wide,
        route_lanes,
        stats,
        True,
        [query, memory, wcross[:, width:], first, both_spots],
        experts,
        length,
    )

    lefts = [low0, mixed0, jnp.where(decoder, low_c, low_m), jnp.where(decoder, mixed_c, low_m)]
    saved = moe_forward(send.reshape(send_shape), w_in, w_down, 1, saved, lefts, rows)
    results = fetch(saved[0])
    final = combine(second, stats, results)
    outputs = final.astype(BF16)

    grad_dec = cotangent[0].reshape(rows, width)
    spread = [(stats[:, GATE + k : GATE + k + 1] * grad_dec.astype(F32)).astype(BF16) for k in range(top)]
    grad_send = dot(spots, jnp.concatenate(spread)).astype(BF16)
    kept_from = moe_backward(grad_send.reshape(experts, block_rows, width), saved, 1, None)

    grad_second, dbranch_c, dgain_moe_dec, dlog_dec, dquery, dmemory = leave(
        cross_info,
        stats,
        gain[1:2],
        router_wide,
        None,
        [
            kept_from[0].reshape(slots, width),
            both,
            grad_dec,
            results,
            second,
            wcross[:, width:],
            mixed_c,
            log_c,
            query,
            memory,
        ],
        experts,
        length,
    )
    dmemory = lax.ppermute(dmemory, names, back_pairs)
    dnormed = dot(dquery, wcross[:, :width], NT)
    dvalues, dgain_c = norm_back(first, scale_c, gain[2], dnormed)
    grad_first_dec = grad_second + dvalues

    grad, grad_send, dgain_m, cross_grad = memory_gradient(
        stats, gain[2:3], [dmemory, wcross, final_enc, grad_dec, spots], [dquery, dbranch_c]
    )
    back, mixed_grads, all_grad = moe_backward(
        grad_send.reshape(experts, block_rows, width), saved, 0, kept_from
    )
    all_rows, hidden, lefts_peer = saved[1], saved[4], saved[10]
    grad_first, dbranch, dgain_moe, dlog, dqkv_rows, diag = leave(
        self_info,
        stats,
        gain[1:2],
        router_wide,
        bias,
        [
            back.reshape(slots, width),
            both,
            grad,
            results,
            second,
            wout,
            mixed0,
            log0,
            qkv,
            grad_first_dec,
        ],
        experts,
        length,
    )
    ff_half = hidden.shape[-1]
    din, ddown = expert_gradients(
        all_rows.reshape(-1, width),
        mixed_grads.reshape(2, -1, ff_half),
        hidden.reshape(-1, ff_half),
        all_grad.reshape(-1, width),
    )
    dlog = jnp.where(decoder, dlog_dec, dlog)[:, FIRST : FIRST + experts]
    dgain_moe = jnp.where(decoder, dgain_moe_dec[0], dgain_moe[0])
    drouter = lax.dot_general(
        second * stats[:, SCALE : SCALE + 1] * gain[1],
        dlog,
        TN,
        precision=lax.Precision.HIGHEST,
        preferred_element_type=F32,
    )
    dnormed = dot(dqkv_rows, wqkv, NT)
    dvalues, dgain_self = norm_back(values, scale0, gain[0], dnormed)
    d_tokens = (grad_first + dvalues).astype(BF16)
    by_entry = lax.dot_general(
        diag, hot_back, NT, precision=lax.Precision.HIGHEST, preferred_element_type=F32
    )
    dtable = jnp.sum(jnp.where(own_head, by_entry, 0.0), axis=0)

    own_grads = (dqkv_rows, dbranch, cross_grad)
    peer_grads = (over_dp(dqkv_rows), over_dp(dbranch), to_neighbour(cross_grad))
    places = 2 * experts
    own = width // places
    extra = jnp.concatenate([dtable.reshape(places, -1), tallies.reshape(places, 1)], axis=1)
    extra = jnp.pad(extra, ((0, 0), (0, -extra.shape[1] % own)))
    small = jnp.concatenate(
        [
            jnp.transpose(drouter),
            jnp.stack([dgain_self, dgain_moe, jnp.where(decoder, dgain_c, dgain_m[0])]),
            jnp.swapaxes(extra.reshape(places, -1, own), 0, 1).reshape(-1, width),
        ]
    )
    small = jnp.pad(small, ((0, -small.shape[0] % 8), (0, 0)))
    (dqkv, dout, dcross), small = dense_gradients(
        lefts, lefts_peer, own_grads, peer_grads, small, experts
    )
    place = lax.axis_index("dp") * experts + lax.axis_index("expert")
    mine = lax.dynamic_slice_in_dim(small, place * own, own, 1)
    tail = mine[experts + 3 :].reshape(-1)
    own_table = dtable.shape[0] // places
    d_table = tail[:own_table]
    counts = tail[own_table].astype(jnp.int32)

    return (
        outputs.reshape(1, seqs, length, width),
        d_tokens.reshape(1, seqs, length, width),
        dqkv[None],
        dout[None],
        dcross[None],
        jnp.transpose(mine[:experts])[None],
        mine[experts : experts + 3][None],
        d_table[None],
        din[None, None],
        ddown[None, None],
        counts.reshape(1, 1, 1),
    )


def half_pairs(count):
    return (
        [(i, count + i) for i in range(count)],
        [(count + i, i) for i in range(count)],
    )


def solution(mesh):
    placed = (
        P("half", ("dp", "expert"), None, None),
        P("half", ("dp", "expert"), None, None),
        P(None, ("dp", "expert")),
        P("half", ("dp", "expert"), None, None),
        P("half", None, None),
        P("half", None, None),
        P("half", None, None),
        P("half", None, None),
        P("half", None, None),
        P("half", None),
        P("half", "expert", None, None, None),
        P("half", "expert", None, None),
    )
    return jax.shard_map(
        body,
        mesh=mesh,
        in_specs=placed,
        out_specs=(
            P("half", ("dp", "expert"), None, None),
            P("half", ("dp", "expert"), None, None),
            P("half", ("dp", "expert"), None),
            P("half", ("dp", "expert"), None),
            P("half", ("dp", "expert"), None),
            P("half", ("dp", "expert"), None),
            P("half", None, ("dp", "expert")),
            P("half", ("dp", "expert")),
            P("half", "expert", None, None, "dp"),
            P("half", "expert", "dp", None),
            P("half", "dp", "expert"),
        ),
        check_vma=False,
    )
```

profile of v0, /device:TPU:0, one launch (start us, length us, event | category | flops | bytes accessed | tf_op | source)
XLA Modules:
  0.0 354.3 jit_solution(10279831539456340711)
XLA Ops:
  0.7 1.4 fusion.43
  5.3 4.7 %fusion.4.refs_0_.refs_9_ = bf16[256,3072]{1,0:T(8,128)(2,1)S(1)} fusion(bf16[256,1024]{1,0:T(8,128)(2,1)S(1)} %bitcast.120, bf16[1,1024,3072]{2,1,0:T(8,128)(2,1)} %param.21), kind=kOutput, calls=%fused_computation.4 | convolution fusion | flops 1611399168 | bytes 8388608 | tf_op jit(solution)/shard_map/dot_general | solution.py:29
  11.7 10.2 %enter_self.1 = (bf16[256,1024]{1,0:T(8,128)(2,1)S(1)}, f32[256,1024]{1,0:T(8,128)S(1)}, f32[256,1024]{1,0:T(8,128)S(1)}, f32[256,128]{1,0:T(8,128)S(1)}, bf16[640,1024]{1,0:T(8,128)(2,1)S(1)}) custom-call(s32[3]{0:T(128)S(1)} %pad_add_fusion.1.info, f32[1,1024]{1,0:T(1,128)S(1)} %get-tuple-element.178.gain_ref, bf16[1024,128]{1,0:T(8,128)(2,1)S(1)} %pad.12.router_ref, ...), custom_call_target="tpu_custom_call" | custom-call | flops 10000000000 | bytes 1048576 | tf_op jit(solution)/shard_map/enter_self/pallas_call | solution.py:782
  23.9 43.7 %moe_forward.2 = (bf16[8,80,1024]{2,1,0:T(8,128)(2,1)}, bf16[2,8,80,1024]{3,2,1,0:T(8,128)(2,1)}, bf16[640,2816]{1,0:T(8,128)(2,1)}, bf16[640,2816]{1,0:T(8,128)...) custom-call(bf16[8,80,1024]{2,1,0:T(8,128)(2,1)} %bitcast.114, ...), custom_call_target="tpu_custom_call" | custom-call | flops 40000000000 | bytes 1048576 | tf_op jit(solution)/shard_map/moe_forward/pallas_call | solution.py:548
  67.6 2.3 fusion.11
  82.4 23.6 %moe_forward.3 = (bf16[8,80,1024]{2,1,0:T(8,128)(2,1)}, bf16[2,8,80,1024]{3,2,1,0:T(8,128)(2,1)}, bf16[640,2816]{1,0:T(8,128)(2,1)}, bf16[640,2816]{1,0:T(8,128)...) custom-call(bf16[8,80,1024]{2,1,0:T(8,128)(2,1)} %bitcast.112, ...), custom_call_target="tpu_custom_call", output_to_operand_aliasing={{0}: (3, {}), {1}: (4, {}), {2}: (5, {}), {3}: (6, {}), {4}... | custom-call | flops 40000000000 | bytes 1048576 | tf_op jit(solution)/shard_map/moe_forward/pallas_call | solution.py:548
  106.1 2.4 convolution_convert_fusion.2
  110.1 1.9 convolution_convert_fusion.1
  112.0 1.9 moe_backward.2
  114.0 2.8 leave_cross.1
  118.5 2.9 multiply_reduce_fusion
  122.7 72.7 %collective-permute-done.1.refs_0_ = bf16[256,2048]{1,0:T(8,128)(2,1)S(1)} collective-permute-done((bf16[256,2048]{1,0:T(8,128)(2,1)}, bf16[256,2048]{1,0:T(8,128)(2,1)S(1)}, u32[]{:S(2)}, u32[]{:S(2)}) %collective-permute-start.1) | collective-permute-done | bytes 1048608 | tf_op jit(solution)/shard_map/ppermute | solution.py:1349
  197.6 2.6 memory_gradient.1
  202.3 42.1 %moe_backward.3 = (bf16[8,80,1024]{2,1,0:T(8,128)(2,1)}, bf16[2,2,640,1408]{3,2,1,0:T(8,128)(2,1)}, bf16[2,8,80,1024]{3,2,1,0:T(8,128)(2,1)}) custom-call(bf16[8,80,1024]{2,1,0:T(8,128)(2,1)} %bitcast.113, bf16[1024,2816]{1,0:T(8,128)(2,1)} %get-tuple-element.97.refs_1_, ...), custom_call_target="tpu_custom_call", output_to_operand_aliasing={{0}: (8, {}), {1}: (9, {}), {2}: (10, {})} | custom-call | flops 40000000000 | bytes 1048576 | tf_op jit(solution)/shard_map/moe_backward/pallas_call | solution.py:548
  244.5 17.3 %leave_self.1 = (f32[256,1024]{1,0:T(8,128)}, bf16[256,1024]{1,0:T(8,128)(2,1)}, f32[8,1024]{1,0:T(8,128)}, f32[256,128]{1,0:T(8,128)}, bf16[256,3072]{1,0:T(8,128)(2,1)}, /*index=5*/f32[16,256]{1,0:T(8,128)}) custom-call(s32[3]{0:T(128)} %copy-done.28, f32[256,128]{1,0:T(8,128)} %copy-done.6, f32[1,1024]{1,0:T(1,128)} %copy-done.15, ...), custom_call_target="tpu_custom_call" | custom-call | flops 16000000000 | bytes 1048576 | tf_op jit(solution)/shard_map/leave_self/pallas_call | solution.py:906
  261.8 6.3 %multiply_reduce_fusion.1 = (f32[1024]{0:T(1024)S(1)}, f32[256]{0:T(256)S(1)}, f32[256,1024]{1,0:T(8,128)}) fusion(f32[256]{0:T(256)S(1)} %copy-done.62, bf16[1,2,128,1024]{3,2,1,0:T(8,128)(2,1)S(1)} %copy-done.1, f32[1024]{0:T(1024)S(1)} %bitcast.127, bf16[256,3072]{1,0:T(8,128)(2,1)} %get-tuple-element.118.refs_4_, bf16[1,1024,3072]{2,1,0:T(8,128)(2,1)} %param.21), kind=kOutput, calls=%fused_computation.30 | convolution fusion | flops 1612446464 | bytes 9447424 | tf_op jit(solution)/shard_map/dot_general | solution.py:29
  268.5 1.7 collective-permute-start.3
  270.8 11.6 %expert_in_gradient.1 = f32[2,1024,1408]{2,1,0:T(8,128)} custom-call(bf16[1280,1024]{1,0:T(8,128)(2,1)S(1)} %bitcast.111, bf16[2,1280,1408]{2,1,0:T(8,128)(2,1)S(1)} %bitcast.108), custom_call_target="tpu_custom_call" | custom-call | flops 12000000000 | bytes 1048576 | tf_op jit(solution)/shard_map/expert_in_gradient/pallas_call | solution.py:1178
  285.6 2.8 add_convert_fusion
  288.4 2.0 copy-done.22
  290.4 6.5 %expert_out_gradient.1 = f32[1408,1024]{1,0:T(8,128)} custom-call(bf16[1280,1408]{1,0:T(8,128)(2,1)S(1)} %bitcast.109, bf16[1280,1024]{1,0:T(8,128)(2,1)S(1)} %bitcast.110), custom_call_target="tpu_custom_call" | custom-call | flops 7000000000 | bytes 1048576 | tf_op jit(solution)/shard_map/expert_out_gradient/pallas_call | solution.py:1191
  297.7 46.4 %dense_gradients.1 = (f32[64,3072]{1,0:T(8,128)}, f32[64,1024]{1,0:T(8,128)}, f32[64,2048]{1,0:T(8,128)}, f32[4,16,1024]{2,1,0:T(8,128)}) custom-call(bf16[256,1024]{1,0:T(8,128)(2,1)} %multiply_convert_fusion.refs_13_.refs_0_, bf16[256,1024]{1,0:T(8,128)(2,1)} %copy-done.44, bf16[256,1024]{1,0:T(8,128)(2,1)} %get-tuple-element.170.refs_15_.refs_2_, ...), custom_call_target="tpu_custom_call" | custom-call | flops 44999999488 | bytes 1048576 | tf_op jit(solution)/shard_map/dense_gradients/pallas_call | solution.py:1151
  348.2 2.1 copy.69
  350.3 1.7 copy.70
  (186 shorter events, 37.0 us)
Async XLA Ops:
  2.1 73.2 %copy-start.54 = (f32[1,1,1024]{2,0,1:T(1,128)}, f32[1,1,1024]{2,0,1:T(1,128)S(1)}, u32[]{:S(2)}) copy-start(f32[1,1,1024]{2,0,1:T(1,128)S(1)} %get-tuple-element.181) | copy-start | bytes 12292
  2.1 75.1 %copy-start.15 = (f32[1,1024]{1,0:T(1,128)}, f32[1,1024]{1,0:T(1,128)S(1)}, u32[]{:S(2)}) copy-start(f32[1,1024]{1,0:T(1,128)S(1)} %get-tuple-element.178.gain_ref) | copy-start | bytes 12292
  3.3 72.0 %copy-start.61 = (f32[256]{0:T(256)}, f32[256]{0:T(256)S(1)}, u32[]{:S(2)}) copy-start(f32[256]{0:T(256)S(1)} %get-tuple-element.183) | copy-start | bytes 3076
  10.2 67.0 %copy-start.13 = (bf16[1024,128]{1,0:T(8,128)(2,1)}, bf16[1024,128]{1,0:T(8,128)(2,1)S(1)}, u32[]{:S(2)}) copy-start(bf16[1024,128]{1,0:T(8,128)(2,1)S(1)} %pad.12.router_ref) | copy-start | bytes 786436
  23.7 43.9 %copy-start.43 = (f32[256,1024]{1,0:T(8,128)}, f32[256,1024]{1,0:T(8,128)S(1)}, u32[]{:S(2)}) copy-start(f32[256,1024]{1,0:T(8,128)S(1)} %get-tuple-element.115.refs_8_) | copy-start | bytes 3145732
  73.6 3.6 %collective-permute-start = (bf16[256,2048]{1,0:T(8,128)(2,1)S(1)}, bf16[256,2048]{1,0:T(8,128)(2,1)S(1)}, u32[]{:S(2)}, u32[]{:S(2)}) collective-permute-start(bf16[256,2048]{1,0:T(8,128)(2,1)S(1)} %convolution_convert_fusion), channel_id=1, source_target_pairs={{0,16},{1,17},{2,18},{3,19},{4,20},{5,21},{6,22},{7,23},{8,24},{9,... | collective-permute-start | bytes 3145736 | tf_op jit(solution)/shard_map/ppermute | solution.py:1300
  81.4 24.6 %copy-start.10 = (bf16[256,1024]{1,0:T(8,128)(2,1)}, bf16[256,1024]{1,0:T(8,128)(2,1)S(1)}, u32[]{:S(2)}) copy-start(bf16[256,1024]{1,0:T(8,128)(2,1)S(1)} %get-tuple-element.94.refs_6_) | copy-start | bytes 1572868
  81.4 27.1 %copy-start.6 = (f32[256,128]{1,0:T(8,128)}, f32[256,128]{1,0:T(8,128)S(1)}, u32[]{:S(2)}) copy-start(f32[256,128]{1,0:T(8,128)S(1)} %get-tuple-element.82.stats_ref) | copy-start | bytes 393220
  116.8 78.6 %collective-permute-start.1 = (bf16[256,2048]{1,0:T(8,128)(2,1)}, bf16[256,2048]{1,0:T(8,128)(2,1)S(1)}, u32[]{:S(2)}, u32[]{:S(2)}) collective-permute-start(bf16[256,2048]{1,0:T(8,128)(2,1)} %get-tuple-element.107), channel_id=1, source_target_pairs={{16,0},{17,1},{18,2},{19,3},{20,4},{21,5},{22,6},{23,7},{24,8},{25... | collective-permute-start | bytes 3145736 | tf_op jit(solution)/shard_map/ppermute | solution.py:1349
  118.5 77.9 %copy-start.9 = (bf16[1,1024,2048]{2,1,0:T(8,128)(2,1)S(1)}, bf16[1,1024,2048]{2,1,0:T(8,128)(2,1)}, u32[]{:S(2)}) copy-start(bf16[1,1024,2048]{2,1,0:T(8,128)(2,1)} %param.23) | copy-start | bytes 12582916
  121.3 75.1 %copy-start.7 = (f32[256,128]{1,0:T(8,128)S(1)}, f32[256,128]{1,0:T(8,128)}, u32[]{:S(2)}) copy-start(f32[256,128]{1,0:T(8,128)} %copy-done.6) | copy-start | bytes 393220
  121.3 75.1 %copy-start.12 = (bf16[1,2,128,1024]{3,2,1,0:T(8,128)(2,1)S(1)}, bf16[1,2,128,1024]{3,2,1,0:T(8,128)(2,1)}, u32[]{:S(2)}) copy-start(bf16[1,2,128,1024]{3,2,1,0:T(8,128)(2,1)} %param.18) | copy-start | bytes 1572868
  121.3 75.1 %copy-start.31 = (bf16[256,1024]{1,0:T(8,128)(2,1)S(1)}, bf16[256,1024]{1,0:T(8,128)(2,1)}, u32[]{:S(2)}) copy-start(bf16[256,1024]{1,0:T(8,128)(2,1)} %get-tuple-element.108.refs_5_) | copy-start | bytes 1572868
  121.4 75.0 %copy-start.34 = (bf16[640,512]{1,0:T(8,128)(2,1)S(1)}, bf16[640,512]{1,0:T(8,128)(2,1)}, u32[]{:S(2)}) copy-start(bf16[640,512]{1,0:T(8,128)(2,1)} %copy-done.32) | copy-start | bytes 1966084
  121.4 75.0 %copy-start.41 = (bf16[256,1024]{1,0:T(8,128)(2,1)S(1)}, bf16[256,1024]{1,0:T(8,128)(2,1)}, u32[]{:S(2)}) copy-start(bf16[256,1024]{1,0:T(8,128)(2,1)} %get-tuple-element.109.refs_6_) | copy-start | bytes 1572868
  202.3 67.8 %copy-start.17 = (bf16[256,2048]{1,0:T(8,128)(2,1)}, bf16[256,2048]{1,0:T(8,128)(2,1)S(1)}, u32[]{:S(2)}) copy-start(bf16[256,2048]{1,0:T(8,128)(2,1)S(1)} %get-tuple-element.120.refs_6_) | copy-start | bytes 3145732
  244.5 17.3 %copy-start.1 = (bf16[1,2,128,1024]{3,2,1,0:T(8,128)(2,1)S(1)}, bf16[1,2,128,1024]{3,2,1,0:T(8,128)(2,1)}, u32[]{:S(2)}) copy-start(bf16[1,2,128,1024]{3,2,1,0:T(8,128)(2,1)} %param.17) | copy-start | bytes 1572868
  244.5 17.3 %copy-start.55 = (f32[1,1,1024]{2,0,1:T(1,128)S(1)}, f32[1,1,1024]{2,0,1:T(1,128)}, u32[]{:S(2)}) copy-start(f32[1,1,1024]{2,0,1:T(1,128)} %copy-done.54) | copy-start | bytes 12292
  244.5 17.3 %copy-start.62 = (f32[256]{0:T(256)S(1)}, f32[256]{0:T(256)}, u32[]{:S(2)}) copy-start(f32[256]{0:T(256)} %copy-done.61) | copy-start | bytes 3076
  268.1 29.6 %collective-permute-start.2 = (bf16[256,3072]{1,0:T(8,128)(2,1)}, bf16[256,3072]{1,0:T(8,128)(2,1)}, u32[]{:S(2)}, u32[]{:S(2)}) collective-permute-start(bf16[256,3072]{1,0:T(8,128)(2,1)} %get-tuple-element.118.refs_4_), channel_id=1, source_target_pairs={{0,8},{8,0},{1,9},{9,1},{2,10},{10,2},{3,11},{11,3},{4,12},{12,4},... | collective-permute-start | bytes 4718600 | tf_op jit(solution)/shard_map/ppermute | solution.py:1129
  268.5 29.2 %collective-permute-start.3 = (bf16[256,1024]{1,0:T(8,128)(2,1)}, bf16[256,1024]{1,0:T(8,128)(2,1)}, u32[]{:S(2)}, u32[]{:S(2)}) collective-permute-start(bf16[256,1024]{1,0:T(8,128)(2,1)} %get-tuple-element.119.refs_5_), channel_id=1, source_target_pairs={{0,8},{8,0},{1,9},{9,1},{2,10},{10,2},{3,11},{11,3},{4,12},{12,4},... | collective-permute-start | bytes 1572872 | tf_op jit(solution)/shard_map/ppermute | solution.py:1129
  270.1 27.5 %collective-permute-start.4 = (bf16[256,2048]{1,0:T(8,128)(2,1)S(1)}, bf16[256,2048]{1,0:T(8,128)(2,1)}, u32[]{:S(2)}, u32[]{:S(2)}) collective-permute-start(bf16[256,2048]{1,0:T(8,128)(2,1)S(1)} %get-tuple-element.120.refs_6_), channel_id=1, source_target_pairs={{0,1},{1,0},{2,3},{3,2},{4,5},{5,4},{6,7},{7,6},{8,9},{9,8},{10,11... | collective-permute-start | bytes 3145736 | tf_op jit(solution)/shard_map/ppermute | solution.py:1125
  270.8 13.1 %copy-start.4 = (f32[256,1024]{1,0:T(8,128)S(1)}, f32[256,1024]{1,0:T(8,128)}, u32[]{:S(2)}) copy-start(f32[256,1024]{1,0:T(8,128)} %copy-done.2) | copy-start | bytes 3145732
  270.8 13.1 %copy-start.52 = (f32[256,128]{1,0:T(8,128)S(1)}, f32[256,128]{1,0:T(8,128)}, u32[]{:S(2)}) copy-start(f32[256,128]{1,0:T(8,128)} %get-tuple-element.122) | copy-start | bytes 393220
  (46 other events, 221.5 us)
where the time goes:
time: 361 us; the launch traced here: 354 us
  Pallas kernels  211 us (58%)
  waiting for transfers between devices  73.6 us (20%)
  local copies, waits for them, and re-layouts  25.4 us (7%)
  matrix products  24.2 us (7%)
  other arithmetic  11.5 us (3%)
  starting transfers between devices  5.27 us (1%)
  between operations  3.77 us (1%)
    pallas_call x4, Pallas kernels, expert_call(): pl.pallas_call(functools.partial(kernel, turn, bool(prev)), in_specs=[vme...  111 us
    ppermute x1, waiting for transfers between devices, body(): dmemory = lax.ppermute(dmemory, names, back_pairs)  72.7 us
    pallas_call x1, Pallas kernels, dense_gradients(): pl.pallas_call(functools.partial(dense_kernel, stages, chunk, 2), in_spec...  46.4 us
    dot_general x8, matrix products, dot(): return lax.dot_general(a, b, dims, preferred_element_type=F32)  22.6 us
    pallas_call x2, Pallas kernels, leave(): pl.pallas_call(functools.partial(leave_kernel, cross, experts, len(source...  20.1 us
    unnamed x136, local copies, waits for them, and re-layouts  19.2 us
    pallas_call x1, Pallas kernels, expert_gradients(): pl.pallas_call(product_kernel, grid=(2, width // tile), in_specs=[pl.Bloc...  11.6 us
    pallas_call x2, Pallas kernels, enter(): pl.pallas_call(functools.partial(enter_kernel, cross, experts, count), in...  11.3 us
  transfers between devices with their start and end apart: 5, of which 3 were waited for; matrix products, arithmetic and copies ran while one was open for 3% of the time, Pallas kernels for 5%

commit v1 on v0

--- a/solution.py
+++ b/solution.py
@@ -197,7 +197,7 @@
         size *= 2
     if experts <= 2 * size:
         half = max(size // 2, 1)
-        return [(0, size), *((k, half) for k in range(size, experts, half))]
+        return [(k, half) for k in range(0, experts, half)]
     return [(k, size) for k in range(0, experts, size)]
 
 
@@ -1173,16 +1173,16 @@
 def expert_gradients(rows, mixed, hidden, grads):
     total, width = rows.shape
     span = hidden.shape[1]
-    tile = 256
+    tile, wide = 256, min(512, width)
     params = pltpu.CompilerParams(vmem_limit_bytes=40 << 20)
     din = pl.pallas_call(
         product_kernel,
-        grid=(2, width // tile),
+        grid=(2, width // wide),
         in_specs=[
-            pl.BlockSpec((total, tile), lambda g, i: (0, i)),
+            pl.BlockSpec((total, wide), lambda g, i: (0, i)),
             pl.BlockSpec((1, total, span), lambda g, i: (g, 0, 0)),
         ],
-        out_specs=pl.BlockSpec((1, tile, span), lambda g, i: (g, i, 0)),
+        out_specs=pl.BlockSpec((1, wide, span), lambda g, i: (g, i, 0)),
         out_shape=jax.ShapeDtypeStruct((2, width, span), F32),
         compiler_params=params,
         cost_estimate=cost(12),

time: 361 us -> 359 us (level)
  Pallas kernels: 211 us -> 205 us
  starting transfers between devices: 5.27 us -> 9.57 us
    pallas_call x4, Pallas kernels: 111 us -> 107 us  [expert_call(): pl.pallas_call(functools.partial(kernel, turn, bool(prev)), in_specs=[vme...]
    ppermute x1, starting transfers between devices: 1.29 us -> 5.19 us  [body(): dmemory = lax.ppermute(dmemory, names, back_pairs)]
  transfers between devices with their start and end apart: 5 -> 5, of which waited for: 3 -> 3; matrix products, arithmetic and copies ran while one was open for 3% -> 4% of each run, Pallas kernels for 5% -> 5%
where the time goes in v1:
time: 359 us; the launch traced here: 353 us
  Pallas kernels  205 us (57%)
  waiting for transfers between devices  73.1 us (20%)
  local copies, waits for them, and re-layouts  25.4 us (7%)
  matrix products  24.2 us (7%)
  other arithmetic  11.5 us (3%)
  starting transfers between devices  9.57 us (3%)
  between operations  3.77 us (1%)
    pallas_call x4, Pallas kernels, expert_call(): pl.pallas_call(functools.partial(kernel, turn, bool(prev)), in_specs=[vme...  107 us
    ppermute x1, waiting for transfers between devices, body(): dmemory = lax.ppermute(dmemory, names, back_pairs)  69.8 us
    pallas_call x1, Pallas kernels, dense_gradients(): pl.pallas_call(functools.partial(dense_kernel, stages, chunk, 2), in_spec...  46.3 us
    dot_general x8, matrix products, dot(): return lax.dot_general(a, b, dims, preferred_element_type=F32)  22.6 us
    pallas_call x2, Pallas kernels, leave(): pl.pallas_call(functools.partial(leave_kernel, cross, experts, len(source...  20.1 us
    unnamed x136, local copies, waits for them, and re-layouts  19.2 us
    pallas_call x2, Pallas kernels, enter(): pl.pallas_call(functools.partial(enter_kernel, cross, experts, count), in...  11.3 us
    pallas_call x1, Pallas kernels, expert_gradients(): pl.pallas_call(product_kernel, grid=(2, width // wide), in_specs=[pl.Bloc...  10.9 us
  transfers between devices with their start and end apart: 5, of which 3 were waited for; matrix products, arithmetic and copies ran while one was open for 4% of the time, Pallas kernels for 5%

profile of v1, /device:TPU:0, one launch (start us, length us, event | category | flops | bytes accessed | tf_op | source)
XLA Modules:
  0.0 352.8 jit_solution(17406094844423730489)
XLA Ops:
  5.3 4.7 %fusion.4.refs_0_.refs_9_ = bf16[256,3072]{1,0:T(8,128)(2,1)S(1)} fusion(bf16[256,1024]{1,0:T(8,128)(2,1)S(1)} %bitcast.120, bf16[1,1024,3072]{2,1,0:T(8,128)(2,1)} %param.21), kind=kOutput, calls=%fused_computation.4 | convolution fusion | flops 1611399168 | bytes 8388608 | tf_op jit(solution)/shard_map/dot_general | solution.py:29
  11.7 10.2 %enter_self.1 = (bf16[256,1024]{1,0:T(8,128)(2,1)S(1)}, f32[256,1024]{1,0:T(8,128)S(1)}, f32[256,1024]{1,0:T(8,128)S(1)}, f32[256,128]{1,0:T(8,128)S(1)}, bf16[640,1024]{1,0:T(8,128)(2,1)S(1)}) custom-call(s32[3]{0:T(128)S(1)} %pad_add_fusion.1.info, f32[1,1024]{1,0:T(1,128)S(1)} %get-tuple-element.178.gain_ref, bf16[1024,128]{1,0:T(8,128)(2,1)S(1)} %pad.12.router_ref, ...), custom_call_target="tpu_custom_call" | custom-call | flops 10000000000 | bytes 1048576 | tf_op jit(solution)/shard_map/enter_self/pallas_call | solution.py:782
  23.9 40.7 %moe_forward.2 = (bf16[8,80,1024]{2,1,0:T(8,128)(2,1)}, bf16[2,8,80,1024]{3,2,1,0:T(8,128)(2,1)}, bf16[640,2816]{1,0:T(8,128)(2,1)}, bf16[640,2816]{1,0:T(8,128)...) custom-call(bf16[8,80,1024]{2,1,0:T(8,128)(2,1)} %bitcast.114, ...), custom_call_target="tpu_custom_call" | custom-call | flops 40000000000 | bytes 1048576 | tf_op jit(solution)/shard_map/moe_forward/pallas_call | solution.py:548
  64.7 2.3 fusion.11
  79.5 23.6 %moe_forward.3 = (bf16[8,80,1024]{2,1,0:T(8,128)(2,1)}, bf16[2,8,80,1024]{3,2,1,0:T(8,128)(2,1)}, bf16[640,2816]{1,0:T(8,128)(2,1)}, bf16[640,2816]{1,0:T(8,128)...) custom-call(bf16[8,80,1024]{2,1,0:T(8,128)(2,1)} %bitcast.112, ...), custom_call_target="tpu_custom_call", output_to_operand_aliasing={{0}: (3, {}), {1}: (4, {}), {2}: (5, {}), {3}: (6, {}), {4}... | custom-call | flops 40000000000 | bytes 1048576 | tf_op jit(solution)/shard_map/moe_forward/pallas_call | solution.py:548
  103.1 2.4 convolution_convert_fusion.2
  107.2 1.9 convolution_convert_fusion.1
  109.1 2.0 moe_backward.2
  111.0 2.8 leave_cross.1
  113.9 5.2 %collective-permute-start.1 = (bf16[256,2048]{1,0:T(8,128)(2,1)}, bf16[256,2048]{1,0:T(8,128)(2,1)S(1)}, u32[]{:S(2)}, u32[]{:S(2)}) collective-permute-start(bf16[256,2048]{1,0:T(8,128)(2,1)} %get-tuple-element.107), channel_id=1, source_target_pairs={{16,0},{17,1},{18,2},{19,3},{20,4},{21,5},{22,6},{23,7},{24,8},{25... | collective-permute-start | bytes 3145736 | tf_op jit(solution)/shard_map/ppermute | solution.py:1349
  119.4 2.9 multiply_reduce_fusion
  123.7 69.8 %collective-permute-done.1.refs_0_ = bf16[256,2048]{1,0:T(8,128)(2,1)S(1)} collective-permute-done((bf16[256,2048]{1,0:T(8,128)(2,1)}, bf16[256,2048]{1,0:T(8,128)(2,1)S(1)}, u32[]{:S(2)}, u32[]{:S(2)}) %collective-permute-start.1) | collective-permute-done | bytes 1048608 | tf_op jit(solution)/shard_map/ppermute | solution.py:1349
  195.7 2.4 memory_gradient.1
  200.2 40.8 %moe_backward.3 = (bf16[8,80,1024]{2,1,0:T(8,128)(2,1)}, bf16[2,2,640,1408]{3,2,1,0:T(8,128)(2,1)}, bf16[2,8,80,1024]{3,2,1,0:T(8,128)(2,1)}) custom-call(bf16[8,80,1024]{2,1,0:T(8,128)(2,1)} %bitcast.113, bf16[1024,2816]{1,0:T(8,128)(2,1)} %get-tuple-element.97.refs_1_, ...), custom_call_target="tpu_custom_call", output_to_operand_aliasing={{0}: (8, {}), {1}: (9, {}), {2}: (10, {})} | custom-call | flops 40000000000 | bytes 1048576 | tf_op jit(solution)/shard_map/moe_backward/pallas_call | solution.py:548
  241.0 17.3 %leave_self.1 = (f32[256,1024]{1,0:T(8,128)}, bf16[256,1024]{1,0:T(8,128)(2,1)}, f32[8,1024]{1,0:T(8,128)}, f32[256,128]{1,0:T(8,128)}, bf16[256,3072]{1,0:T(8,128)(2,1)}, /*index=5*/f32[16,256]{1,0:T(8,128)}) custom-call(s32[3]{0:T(128)} %copy-done.28, f32[256,128]{1,0:T(8,128)} %copy-done.6, f32[1,1024]{1,0:T(1,128)} %copy-done.15, ...), custom_call_target="tpu_custom_call" | custom-call | flops 16000000000 | bytes 1048576 | tf_op jit(solution)/shard_map/leave_self/pallas_call | solution.py:906
  258.4 6.3 %multiply_reduce_fusion.1 = (f32[1024]{0:T(1024)S(1)}, f32[256]{0:T(256)S(1)}, f32[256,1024]{1,0:T(8,128)}) fusion(f32[256]{0:T(256)S(1)} %copy-done.62, bf16[1,2,128,1024]{3,2,1,0:T(8,128)(2,1)S(1)} %copy-done.1, f32[1024]{0:T(1024)S(1)} %bitcast.127, bf16[256,3072]{1,0:T(8,128)(2,1)} %get-tuple-element.118.refs_4_, bf16[1,1024,3072]{2,1,0:T(8,128)(2,1)} %param.21), kind=kOutput, calls=%fused_computation.30 | convolution fusion | flops 1612446464 | bytes 9447424 | tf_op jit(solution)/shard_map/dot_general | solution.py:29
  267.8 10.9 %expert_in_gradient.1 = f32[2,1024,1408]{2,1,0:T(8,128)} custom-call(bf16[1280,1024]{1,0:T(8,128)(2,1)S(1)} %bitcast.111, bf16[2,1280,1408]{2,1,0:T(8,128)(2,1)S(1)} %bitcast.108), custom_call_target="tpu_custom_call" | custom-call | flops 12000000000 | bytes 1048576 | tf_op jit(solution)/shard_map/expert_in_gradient/pallas_call | solution.py:1178
  281.8 2.8 add_convert_fusion
  284.6 2.0 copy-done.22
  286.6 6.5 %expert_out_gradient.1 = f32[1408,1024]{1,0:T(8,128)} custom-call(bf16[1280,1408]{1,0:T(8,128)(2,1)S(1)} %bitcast.109, bf16[1280,1024]{1,0:T(8,128)(2,1)S(1)} %bitcast.110), custom_call_target="tpu_custom_call" | custom-call | flops 7000000000 | bytes 1048576 | tf_op jit(solution)/shard_map/expert_out_gradient/pallas_call | solution.py:1191
  293.1 3.2 collective-permute-done.3.refs_8_
  296.3 46.3 %dense_gradients.1 = (f32[64,3072]{1,0:T(8,128)}, f32[64,1024]{1,0:T(8,128)}, f32[64,2048]{1,0:T(8,128)}, f32[4,16,1024]{2,1,0:T(8,128)}) custom-call(bf16[256,1024]{1,0:T(8,128)(2,1)} %multiply_convert_fusion.refs_13_.refs_0_, bf16[256,1024]{1,0:T(8,128)(2,1)} %copy-done.44, bf16[256,1024]{1,0:T(8,128)(2,1)} %get-tuple-element.170.refs_15_.refs_2_, ...), custom_call_target="tpu_custom_call" | custom-call | flops 44999999488 | bytes 1048576 | tf_op jit(solution)/shard_map/dense_gradients/pallas_call | solution.py:1151
  346.7 2.1 copy.69
  348.8 1.7 copy.70
  (186 shorter events, 38.3 us)
Async XLA Ops:
  2.1 70.2 %copy-start.54 = (f32[1,1,1024]{2,0,1:T(1,128)}, f32[1,1,1024]{2,0,1:T(1,128)S(1)}, u32[]{:S(2)}) copy-start(f32[1,1,1024]{2,0,1:T(1,128)S(1)} %get-tuple-element.181) | copy-start | bytes 12292
  2.1 72.2 %copy-start.15 = (f32[1,1024]{1,0:T(1,128)}, f32[1,1024]{1,0:T(1,128)S(1)}, u32[]{:S(2)}) copy-start(f32[1,1024]{1,0:T(1,128)S(1)} %get-tuple-element.178.gain_ref) | copy-start | bytes 12292
  3.3 69.0 %copy-start.61 = (f32[256]{0:T(256)}, f32[256]{0:T(256)S(1)}, u32[]{:S(2)}) copy-start(f32[256]{0:T(256)S(1)} %get-tuple-element.183) | copy-start | bytes 3076
  10.2 64.0 %copy-start.13 = (bf16[1024,128]{1,0:T(8,128)(2,1)}, bf16[1024,128]{1,0:T(8,128)(2,1)S(1)}, u32[]{:S(2)}) copy-start(bf16[1024,128]{1,0:T(8,128)(2,1)S(1)} %pad.12.router_ref) | copy-start | bytes 786436
  23.7 40.9 %copy-start.43 = (f32[256,1024]{1,0:T(8,128)}, f32[256,1024]{1,0:T(8,128)S(1)}, u32[]{:S(2)}) copy-start(f32[256,1024]{1,0:T(8,128)S(1)} %get-tuple-element.115.refs_8_) | copy-start | bytes 3145732
  70.6 3.6 %collective-permute-start = (bf16[256,2048]{1,0:T(8,128)(2,1)S(1)}, bf16[256,2048]{1,0:T(8,128)(2,1)S(1)}, u32[]{:S(2)}, u32[]{:S(2)}) collective-permute-start(bf16[256,2048]{1,0:T(8,128)(2,1)S(1)} %convolution_convert_fusion), channel_id=1, source_target_pairs={{0,16},{1,17},{2,18},{3,19},{4,20},{5,21},{6,22},{7,23},{8,24},{9,... | collective-permute-start | bytes 3145736 | tf_op jit(solution)/shard_map/ppermute | solution.py:1300
  78.5 24.6 %copy-start.10 = (bf16[256,1024]{1,0:T(8,128)(2,1)}, bf16[256,1024]{1,0:T(8,128)(2,1)S(1)}, u32[]{:S(2)}) copy-start(bf16[256,1024]{1,0:T(8,128)(2,1)S(1)} %get-tuple-element.94.refs_6_) | copy-start | bytes 1572868
  78.5 27.1 %copy-start.6 = (f32[256,128]{1,0:T(8,128)}, f32[256,128]{1,0:T(8,128)S(1)}, u32[]{:S(2)}) copy-start(f32[256,128]{1,0:T(8,128)S(1)} %get-tuple-element.82.stats_ref) | copy-start | bytes 393220
  113.9 79.6 %collective-permute-start.1 = (bf16[256,2048]{1,0:T(8,128)(2,1)}, bf16[256,2048]{1,0:T(8,128)(2,1)S(1)}, u32[]{:S(2)}, u32[]{:S(2)}) collective-permute-start(bf16[256,2048]{1,0:T(8,128)(2,1)} %get-tuple-element.107), channel_id=1, source_target_pairs={{16,0},{17,1},{18,2},{19,3},{20,4},{21,5},{22,6},{23,7},{24,8},{25... | collective-permute-start | bytes 3145736 | tf_op jit(solution)/shard_map/ppermute | solution.py:1349
  119.4 75.0 %copy-start.9 = (bf16[1,1024,2048]{2,1,0:T(8,128)(2,1)S(1)}, bf16[1,1024,2048]{2,1,0:T(8,128)(2,1)}, u32[]{:S(2)}) copy-start(bf16[1,1024,2048]{2,1,0:T(8,128)(2,1)} %param.23) | copy-start | bytes 12582916
  122.3 72.2 %copy-start.7 = (f32[256,128]{1,0:T(8,128)S(1)}, f32[256,128]{1,0:T(8,128)}, u32[]{:S(2)}) copy-start(f32[256,128]{1,0:T(8,128)} %copy-done.6) | copy-start | bytes 393220
  122.3 72.2 %copy-start.12 = (bf16[1,2,128,1024]{3,2,1,0:T(8,128)(2,1)S(1)}, bf16[1,2,128,1024]{3,2,1,0:T(8,128)(2,1)}, u32[]{:S(2)}) copy-start(bf16[1,2,128,1024]{3,2,1,0:T(8,128)(2,1)} %param.18) | copy-start | bytes 1572868
  122.3 72.1 %copy-start.31 = (bf16[256,1024]{1,0:T(8,128)(2,1)S(1)}, bf16[256,1024]{1,0:T(8,128)(2,1)}, u32[]{:S(2)}) copy-start(bf16[256,1024]{1,0:T(8,128)(2,1)} %get-tuple-element.108.refs_5_) | copy-start | bytes 1572868
  122.3 72.1 %copy-start.34 = (bf16[640,512]{1,0:T(8,128)(2,1)S(1)}, bf16[640,512]{1,0:T(8,128)(2,1)}, u32[]{:S(2)}) copy-start(bf16[640,512]{1,0:T(8,128)(2,1)} %copy-done.32) | copy-start | bytes 1966084
  122.3 72.1 %copy-start.41 = (bf16[256,1024]{1,0:T(8,128)(2,1)S(1)}, bf16[256,1024]{1,0:T(8,128)(2,1)}, u32[]{:S(2)}) copy-start(bf16[256,1024]{1,0:T(8,128)(2,1)} %get-tuple-element.109.refs_6_) | copy-start | bytes 1572868
  200.2 66.5 %copy-start.17 = (bf16[256,2048]{1,0:T(8,128)(2,1)}, bf16[256,2048]{1,0:T(8,128)(2,1)S(1)}, u32[]{:S(2)}) copy-start(bf16[256,2048]{1,0:T(8,128)(2,1)S(1)} %get-tuple-element.120.refs_6_) | copy-start | bytes 3145732
  241.0 17.3 %copy-start.1 = (bf16[1,2,128,1024]{3,2,1,0:T(8,128)(2,1)S(1)}, bf16[1,2,128,1024]{3,2,1,0:T(8,128)(2,1)}, u32[]{:S(2)}) copy-start(bf16[1,2,128,1024]{3,2,1,0:T(8,128)(2,1)} %param.17) | copy-start | bytes 1572868
  241.0 17.3 %copy-start.55 = (f32[1,1,1024]{2,0,1:T(1,128)S(1)}, f32[1,1,1024]{2,0,1:T(1,128)}, u32[]{:S(2)}) copy-start(f32[1,1,1024]{2,0,1:T(1,128)} %copy-done.54) | copy-start | bytes 12292
  241.0 17.3 %copy-start.62 = (f32[256]{0:T(256)S(1)}, f32[256]{0:T(256)}, u32[]{:S(2)}) copy-start(f32[256]{0:T(256)} %copy-done.61) | copy-start | bytes 3076
  264.7 31.7 %collective-permute-start.2 = (bf16[256,3072]{1,0:T(8,128)(2,1)}, bf16[256,3072]{1,0:T(8,128)(2,1)}, u32[]{:S(2)}, u32[]{:S(2)}) collective-permute-start(bf16[256,3072]{1,0:T(8,128)(2,1)} %get-tuple-element.118.refs_4_), channel_id=1, source_target_pairs={{0,8},{8,0},{1,9},{9,1},{2,10},{10,2},{3,11},{11,3},{4,12},{12,4},... | collective-permute-start | bytes 4718600 | tf_op jit(solution)/shard_map/ppermute | solution.py:1129
  266.0 30.3 %collective-permute-start.3 = (bf16[256,1024]{1,0:T(8,128)(2,1)}, bf16[256,1024]{1,0:T(8,128)(2,1)}, u32[]{:S(2)}, u32[]{:S(2)}) collective-permute-start(bf16[256,1024]{1,0:T(8,128)(2,1)} %get-tuple-element.119.refs_5_), channel_id=1, source_target_pairs={{0,8},{8,0},{1,9},{9,1},{2,10},{10,2},{3,11},{11,3},{4,12},{12,4},... | collective-permute-start | bytes 1572872 | tf_op jit(solution)/shard_map/ppermute | solution.py:1129
  266.7 29.6 %collective-permute-start.4 = (bf16[256,2048]{1,0:T(8,128)(2,1)S(1)}, bf16[256,2048]{1,0:T(8,128)(2,1)}, u32[]{:S(2)}, u32[]{:S(2)}) collective-permute-start(bf16[256,2048]{1,0:T(8,128)(2,1)S(1)} %get-tuple-element.120.refs_6_), channel_id=1, source_target_pairs={{0,1},{1,0},{2,3},{3,2},{4,5},{5,4},{6,7},{7,6},{8,9},{9,8},{10,11... | collective-permute-start | bytes 3145736 | tf_op jit(solution)/shard_map/ppermute | solution.py:1125
  267.7 12.4 %copy-start.4 = (f32[256,1024]{1,0:T(8,128)S(1)}, f32[256,1024]{1,0:T(8,128)}, u32[]{:S(2)}) copy-start(f32[256,1024]{1,0:T(8,128)} %copy-done.2) | copy-start | bytes 3145732
  267.7 12.4 %copy-start.52 = (f32[256,128]{1,0:T(8,128)S(1)}, f32[256,128]{1,0:T(8,128)}, u32[]{:S(2)}) copy-start(f32[256,128]{1,0:T(8,128)} %get-tuple-element.122) | copy-start | bytes 393220
  (46 other events, 217.8 us)
